TPU v7x, 128 devices: a whole 4x4x4 slice. The times are simulated.
128 devices in a mesh: stretch: 16 (over z, x_lo, core), grp: 8 (over x_hi, y).
Axes of the slice: x: 4 (x_hi: 2, x_lo: 2; x = x_hi * 2 + x_lo), y: 4, z: 4, core: 2. Of those that a mesh axis runs over, the one named last changes fastest.
Arguments:
- queries: bfloat16 [16384, 4096], P(('stretch', 'grp')), may hold values from -6 to 6
- keys: bfloat16 [16384, 4096], P(('stretch', 'grp')), may hold values from -6 to 6
- values: bfloat16 [16384, 4096], P(('stretch', 'grp')), may hold values from -6 to 6
- short_filter: float32 [3, 3, 4096], replicated, may hold values from -3 to 3
- long_filter: bfloat16 [3072, 4096], P(None, 'grp'), may hold values from -0.109375 to 0.109375
- skip_gain: float32 [4096], P('grp'), may hold values from -4 to 4
Outputs:
- filtered: bfloat16 [16384, 4096], P('stretch', 'grp')
All inputs are finite; a program needn't handle non-finite values.
Results may differ from a plain program's by a relative error of at most 0.012.
Values may be sent and summed in bfloat16 or wider, within the bound.
A program may use at most 128 MiB of HBM per device.

v0:
```python
import jax
import jax.numpy as jnp
from jax import lax
from jax.sharding import PartitionSpec as P


def passed_along(block, axis, distance):
    devices = range(lax.axis_size(axis))
    route = [(i - distance, i) for i in devices if i - distance in devices]
    return lax.ppermute(block, axis, route)


def transform_tables(block_len):
    period = 2 * block_len
    sample_index = jnp.arange(period, dtype=jnp.int32)
    bin_number = jnp.where(sample_index < block_len, sample_index, sample_index - block_len)
    phases = sample_index[:, None] * bin_number[None, :] % period
    angles = 2.0 * jnp.pi / period * phases.astype(jnp.float32)
    cosine = jnp.cos(angles)
    sine_table = jnp.sin(angles)
    parity = jnp.where(sample_index % 2 == 0, 1.0, -1.0).astype(jnp.float32)
    is_real = (sample_index < block_len)[None, :]
    is_top = (sample_index == block_len)[None, :]
    forward = jnp.where(is_real, cosine, jnp.where(is_top, parity[:, None], -sine_table))[
        :block_len
    ]
    coefficient = jnp.where(sample_index == 0, 1.0, 2.0).astype(jnp.float32)[:, None]
    inverse = jnp.where(
        is_real.T, coefficient * cosine.T, jnp.where(is_top.T, parity[None, :], -2.0 * sine_table.T)
    )
    return (forward, inverse / period)


def packed_product(filter_bins, signal_bins, first_bin):
    halfway = filter_bins.shape[-1] // 2
    filter_real, filter_imag = (filter_bins[..., :halfway], filter_bins[..., halfway:])
    signal_real, signal_imag = (signal_bins[..., :halfway], signal_bins[..., halfway:])
    real_part = filter_real * signal_real - (1.0 - first_bin) * filter_imag * signal_imag
    imag_part = first_bin * filter_imag * signal_imag + (1.0 - first_bin) * (
        filter_real * signal_imag + filter_imag * signal_real
    )
    return jnp.concatenate([real_part, imag_part], axis=-1)


def earlier_pieces(payload):
    return [passed_along(payload, "stretch", distance) for distance in (3, 2, 1)]


def local(queries, keys, values, short_filter, long_filter, skip_gain):
    tok_rows = queries.shape[0]
    rim_rows = passed_along(
        (queries[tok_rows - 2 :], keys[tok_rows - 2 :], values[tok_rows - 2 :]),
        ("stretch", "grp"),
        1,
    )

    def shorten(current, previous, position):
        joined = jnp.concatenate(
            [previous.astype(jnp.float32), current.astype(jnp.float32)], axis=0
        )
        return (
            short_filter[0, position] * joined[2:]
            + short_filter[1, position] * joined[1:-1]
            + short_filter[2, position] * joined[:-2]
        )

    q_short = shorten(queries, rim_rows[0], 0).astype(jnp.bfloat16)
    gated = (shorten(keys, rim_rows[1], 1) * shorten(values, rim_rows[2], 2)).astype(jnp.bfloat16)
    q_slices, gated_slices = (
        lax.all_to_all(q_short, "grp", split_axis=1, concat_axis=0, tiled=True),
        lax.all_to_all(gated, "grp", split_axis=1, concat_axis=0, tiled=True),
    )
    piece_len, channels = gated_slices.shape
    block_len = min(256, piece_len)
    per_piece = piece_len // block_len
    filter_blocks = long_filter.shape[0] // block_len
    forward, inverse = transform_tables(block_len)

    def spectra(signal):
        blocks = signal.astype(jnp.float32).reshape(-1, block_len, channels)
        return jnp.einsum("jbc,bf->jcf", blocks, forward, precision=lax.Precision.HIGH)

    window = spectra(jnp.concatenate(earlier_pieces(gated_slices) + [gated_slices], axis=0))
    filter_bins = spectra(long_filter)
    first_bin = (jnp.arange(block_len) == 0).astype(jnp.float32)
    outputs = per_piece + 1

    def accumulate(offset, totals):
        filter_slice = lax.dynamic_index_in_dim(filter_bins, offset, 0, keepdims=False)
        inputs = lax.dynamic_slice_in_dim(window, filter_blocks - 1 - offset, outputs, 0)
        return totals + packed_product(filter_slice[None], inputs, first_bin)

    totals = lax.fori_loop(
        0, filter_blocks, accumulate, jnp.zeros((outputs, channels, 2 * block_len), jnp.float32)
    )
    spans = jnp.einsum("kcf,ft->ktc", totals, inverse, precision=lax.Precision.HIGH)
    convolved = (spans[1:, :block_len] + spans[:-1, block_len:]).reshape(piece_len, channels)
    result = q_slices.astype(jnp.float32) * (
        convolved + skip_gain * gated_slices.astype(jnp.float32)
    )
    return result.astype(jnp.bfloat16)


def solution(mesh):
    return jax.shard_map(
        local,
        mesh=mesh,
        in_specs=(
            P(("stretch", "grp"), None),
            P(("stretch", "grp"), None),
            P(("stretch", "grp"), None),
            P(),
            P(None, "grp"),
            P("grp"),
        ),
        out_specs=P("stretch", "grp"),
        check_vma=False,
    )
```

profile of v0, /device:TPU:96, one launch (start us, length us, event | category | flops | bytes accessed | tf_op | source)
XLA Modules:
  0.0 288.8 jit_solution(2921002344506120103)
XLA Ops:
  18.6 5.7 %all-to-all-start.1 = ((bf16[128,8,512]{2,0,1:T(8,128)(2,1)}), bf16[128,8,512]{2,0,1:T(8,128)(2,1)}, u32[]{:S(2)}, u32[]{:S(2)}) async-start(bf16[128,8,512]{2,0,1:T(8,128)(2,1)} %bitcast.61), calls=%async_computation.1 | async-start | bytes 2097152 | tf_op jit(solution)/shard_map/all_to_all | solution.py:71
  25.7 10.2 %convolution_bitcast_fusion = f32[12,512,512]{2,1,0:T(8,128)} fusion(bf16[12,256,512]{2,1,0:T(8,128)(2,1)S(1)} %bitcast.58, s32[512,512]{0,1:T(8,128)S(1)} %add_select_fusion, f32[256]{0:T(256)S(1)} %slice.137, pred[512]{0:T(512)(128)(4,1)S(1)} %get-tuple-element.200, pred[512]{0:T(512)(128)(4,1)S(1)} %get-tuple-element.199), kind=kOutput, calls=%fused_computation.10 | convolution fusion | flops 4832493568 | bytes 16254976 | tf_op jit(solution)/shard_map/jbc,bf->jcf/dot_general | solution.py:81
  53.7 47.4 %collective-permute-done.3 = bf16[1024,512]{1,0:T(8,128)(2,1)} collective-permute-done((bf16[1024,512]{1,0:T(8,128)(2,1)}, bf16[1024,512]{1,0:T(8,128)(2,1)}, u32[]{:S(2)}, u32[]{:S(2)}) %collective-permute-start.3) | collective-permute-done | bytes 1048608 | tf_op jit(solution)/shard_map/ppermute | solution.py:10
  103.4 12.3 %fusion.43 = f32[16,512,512]{2,1,0:T(8,128)} fusion(bf16[16,256,512]{2,1,0:T(8,128)(2,1)S(1)} %bitcast.59, s32[512,512]{0,1:T(8,128)S(1)} %copy-done.3, f32[256]{0:T(256)S(1)} %slice.137, pred[512]{0:T(512)(128)(4,1)S(1)} %get-tuple-element.200, pred[512]{0:T(512)(128)(4,1)S(1)} %get-tuple-element.199), kind=kOutput, calls=%fused_computation.72 | convolution fusion | flops 6443106304 | bytes 21497856 | tf_op jit(solution)/shard_map/jbc,bf->jcf/dot_general | solution.py:81
  115.8 156.4 %while.17 = (s32[]{:T(128)}, f32[5,512,512]{2,1,0:T(8,128)}, f32[12,512,512]{2,1,0:T(8,128)}, f32[16,512,512]{2,1,0:T(8,128)}, s32[]{:T(128)}, /*index=5*/s32[]{:T(128)}, s32[]{:T(128)}, s32[]{:T(128)}, s32[]{}) while((s32[]{:T(128)}, f32[5,512,512]{2,1,0:T(8,128)}, f32[12,512,512]{2,1,0:T(8,128)}, ...), condition=%wide.region_1.2_spmd.clone.clone, body=%wide.region_0.1_spmd.clone.clone.sunk | while | flops 10093832 | bytes 31462576 | solution.py:93
  117.1 4.8 %multiply_subtract_fusion.2 = (f32[5,512,256]{2,1,0:T(8,128)S(1)}, f32[5,512,256]{2,1,0:T(8,128)}) fusion(f32[16,512,512]{2,1,0:T(8,128)} %get-tuple-element.259, s32[]{:T(128)S(6)} %select_n.157, s32[]{:T(128)S(6)} %add.207, f32[512,256]{1,0:T(8,128)S(1)} %get-tuple-element.232, f32[512,256]{1,0:T(8,128)S(1)} %get-tuple-element.233, ...), kind=kLoop, calls=%fused_computation.3.clone.1 | loop fusion | flops 5898240 | bytes 12583944 | tf_op jit(solution)/shard_map/while/body/eval_jaxpr/sub | solution.py:38
  122.0 5.4 %maximum_add_fusion.2 = f32[5,512,512]{2,1,0:T(8,128)} fusion(f32[5,512,256]{2,1,0:T(8,128)} %get-tuple-element.236, f32[5,512,256]{2,1,0:T(8,128)S(1)} %get-tuple-element.237, f32[5,512,512]{2,1,0:T(8,128)} %get-tuple-element.248, pred[]{:T(512)S(6)} %compare.7), kind=kLoop, calls=%fused_computation.1.clone.1 | loop fusion | flops 3932160 | bytes 15728641 | tf_op jit(solution)/shard_map/while/body/eval_jaxpr/add | solution.py:91
  128.7 4.8 %multiply_subtract_fusion.2 = (f32[5,512,256]{2,1,0:T(8,128)S(1)}, f32[5,512,256]{2,1,0:T(8,128)}) fusion(f32[16,512,512]{2,1,0:T(8,128)} %get-tuple-element.259, s32[]{:T(128)S(6)} %select_n.157, s32[]{:T(128)S(6)} %add.207, f32[512,256]{1,0:T(8,128)S(1)} %get-tuple-element.232, f32[512,256]{1,0:T(8,128)S(1)} %get-tuple-element.233, ...), kind=kLoop, calls=%fused_computation.3.clone.1 | loop fusion | flops 5898240 | bytes 12583944 | tf_op jit(solution)/shard_map/while/body/eval_jaxpr/sub | solution.py:38
  133.6 7.0 %maximum_add_fusion.2 = f32[5,512,512]{2,1,0:T(8,128)} fusion(f32[5,512,256]{2,1,0:T(8,128)} %get-tuple-element.236, f32[5,512,256]{2,1,0:T(8,128)S(1)} %get-tuple-element.237, f32[5,512,512]{2,1,0:T(8,128)} %get-tuple-element.248, pred[]{:T(512)S(6)} %compare.7), kind=kLoop, calls=%fused_computation.1.clone.1 | loop fusion | flops 3932160 | bytes 15728641 | tf_op jit(solution)/shard_map/while/body/eval_jaxpr/add | solution.py:91
  141.9 4.8 %multiply_subtract_fusion.2 = (f32[5,512,256]{2,1,0:T(8,128)S(1)}, f32[5,512,256]{2,1,0:T(8,128)}) fusion(f32[16,512,512]{2,1,0:T(8,128)} %get-tuple-element.259, s32[]{:T(128)S(6)} %select_n.157, s32[]{:T(128)S(6)} %add.207, f32[512,256]{1,0:T(8,128)S(1)} %get-tuple-element.232, f32[512,256]{1,0:T(8,128)S(1)} %get-tuple-element.233, ...), kind=kLoop, calls=%fused_computation.3.clone.1 | loop fusion | flops 5898240 | bytes 12583944 | tf_op jit(solution)/shard_map/while/body/eval_jaxpr/sub | solution.py:38
  146.7 7.0 %maximum_add_fusion.2 = f32[5,512,512]{2,1,0:T(8,128)} fusion(f32[5,512,256]{2,1,0:T(8,128)} %get-tuple-element.236, f32[5,512,256]{2,1,0:T(8,128)S(1)} %get-tuple-element.237, f32[5,512,512]{2,1,0:T(8,128)} %get-tuple-element.248, pred[]{:T(512)S(6)} %compare.7), kind=kLoop, calls=%fused_computation.1.clone.1 | loop fusion | flops 3932160 | bytes 15728641 | tf_op jit(solution)/shard_map/while/body/eval_jaxpr/add | solution.py:91
  155.1 4.8 %multiply_subtract_fusion.2 = (f32[5,512,256]{2,1,0:T(8,128)S(1)}, f32[5,512,256]{2,1,0:T(8,128)}) fusion(f32[16,512,512]{2,1,0:T(8,128)} %get-tuple-element.259, s32[]{:T(128)S(6)} %select_n.157, s32[]{:T(128)S(6)} %add.207, f32[512,256]{1,0:T(8,128)S(1)} %get-tuple-element.232, f32[512,256]{1,0:T(8,128)S(1)} %get-tuple-element.233, ...), kind=kLoop, calls=%fused_computation.3.clone.1 | loop fusion | flops 5898240 | bytes 12583944 | tf_op jit(solution)/shard_map/while/body/eval_jaxpr/sub | solution.py:38
  159.9 7.0 %maximum_add_fusion.2 = f32[5,512,512]{2,1,0:T(8,128)} fusion(f32[5,512,256]{2,1,0:T(8,128)} %get-tuple-element.236, f32[5,512,256]{2,1,0:T(8,128)S(1)} %get-tuple-element.237, f32[5,512,512]{2,1,0:T(8,128)} %get-tuple-element.248, pred[]{:T(512)S(6)} %compare.7), kind=kLoop, calls=%fused_computation.1.clone.1 | loop fusion | flops 3932160 | bytes 15728641 | tf_op jit(solution)/shard_map/while/body/eval_jaxpr/add | solution.py:91
  168.2 4.8 %multiply_subtract_fusion.2 = (f32[5,512,256]{2,1,0:T(8,128)S(1)}, f32[5,512,256]{2,1,0:T(8,128)}) fusion(f32[16,512,512]{2,1,0:T(8,128)} %get-tuple-element.259, s32[]{:T(128)S(6)} %select_n.157, s32[]{:T(128)S(6)} %add.207, f32[512,256]{1,0:T(8,128)S(1)} %get-tuple-element.232, f32[512,256]{1,0:T(8,128)S(1)} %get-tuple-element.233, ...), kind=kLoop, calls=%fused_computation.3.clone.1 | loop fusion | flops 5898240 | bytes 12583944 | tf_op jit(solution)/shard_map/while/body/eval_jaxpr/sub | solution.py:38
  173.1 7.0 %maximum_add_fusion.2 = f32[5,512,512]{2,1,0:T(8,128)} fusion(f32[5,512,256]{2,1,0:T(8,128)} %get-tuple-element.236, f32[5,512,256]{2,1,0:T(8,128)S(1)} %get-tuple-element.237, f32[5,512,512]{2,1,0:T(8,128)} %get-tuple-element.248, pred[]{:T(512)S(6)} %compare.7), kind=kLoop, calls=%fused_computation.1.clone.1 | loop fusion | flops 3932160 | bytes 15728641 | tf_op jit(solution)/shard_map/while/body/eval_jaxpr/add | solution.py:91
  181.4 4.8 %multiply_subtract_fusion.2 = (f32[5,512,256]{2,1,0:T(8,128)S(1)}, f32[5,512,256]{2,1,0:T(8,128)}) fusion(f32[16,512,512]{2,1,0:T(8,128)} %get-tuple-element.259, s32[]{:T(128)S(6)} %select_n.157, s32[]{:T(128)S(6)} %add.207, f32[512,256]{1,0:T(8,128)S(1)} %get-tuple-element.232, f32[512,256]{1,0:T(8,128)S(1)} %get-tuple-element.233, ...), kind=kLoop, calls=%fused_computation.3.clone.1 | loop fusion | flops 5898240 | bytes 12583944 | tf_op jit(solution)/shard_map/while/body/eval_jaxpr/sub | solution.py:38
  186.2 7.0 %maximum_add_fusion.2 = f32[5,512,512]{2,1,0:T(8,128)} fusion(f32[5,512,256]{2,1,0:T(8,128)} %get-tuple-element.236, f32[5,512,256]{2,1,0:T(8,128)S(1)} %get-tuple-element.237, f32[5,512,512]{2,1,0:T(8,128)} %get-tuple-element.248, pred[]{:T(512)S(6)} %compare.7), kind=kLoop, calls=%fused_computation.1.clone.1 | loop fusion | flops 3932160 | bytes 15728641 | tf_op jit(solution)/shard_map/while/body/eval_jaxpr/add | solution.py:91
  199.4 7.0 %maximum_add_fusion.2 = f32[5,512,512]{2,1,0:T(8,128)} fusion(f32[5,512,256]{2,1,0:T(8,128)} %get-tuple-element.236, f32[5,512,256]{2,1,0:T(8,128)S(1)} %get-tuple-element.237, f32[5,512,512]{2,1,0:T(8,128)} %get-tuple-element.248, pred[]{:T(512)S(6)} %compare.7), kind=kLoop, calls=%fused_computation.1.clone.1 | loop fusion | flops 3932160 | bytes 15728641 | tf_op jit(solution)/shard_map/while/body/eval_jaxpr/add | solution.py:91
  212.6 7.0 %maximum_add_fusion.2 = f32[5,512,512]{2,1,0:T(8,128)} fusion(f32[5,512,256]{2,1,0:T(8,128)} %get-tuple-element.236, f32[5,512,256]{2,1,0:T(8,128)S(1)} %get-tuple-element.237, f32[5,512,512]{2,1,0:T(8,128)} %get-tuple-element.248, pred[]{:T(512)S(6)} %compare.7), kind=kLoop, calls=%fused_computation.1.clone.1 | loop fusion | flops 3932160 | bytes 15728641 | tf_op jit(solution)/shard_map/while/body/eval_jaxpr/add | solution.py:91
  225.7 7.0 %maximum_add_fusion.2 = f32[5,512,512]{2,1,0:T(8,128)} fusion(f32[5,512,256]{2,1,0:T(8,128)} %get-tuple-element.236, f32[5,512,256]{2,1,0:T(8,128)S(1)} %get-tuple-element.237, f32[5,512,512]{2,1,0:T(8,128)} %get-tuple-element.248, pred[]{:T(512)S(6)} %compare.7), kind=kLoop, calls=%fused_computation.1.clone.1 | loop fusion | flops 3932160 | bytes 15728641 | tf_op jit(solution)/shard_map/while/body/eval_jaxpr/add | solution.py:91
  238.9 7.0 %maximum_add_fusion.2 = f32[5,512,512]{2,1,0:T(8,128)} fusion(f32[5,512,256]{2,1,0:T(8,128)} %get-tuple-element.236, f32[5,512,256]{2,1,0:T(8,128)S(1)} %get-tuple-element.237, f32[5,512,512]{2,1,0:T(8,128)} %get-tuple-element.248, pred[]{:T(512)S(6)} %compare.7), kind=kLoop, calls=%fused_computation.1.clone.1 | loop fusion | flops 3932160 | bytes 15728641 | tf_op jit(solution)/shard_map/while/body/eval_jaxpr/add | solution.py:91
  252.1 7.0 %maximum_add_fusion.2 = f32[5,512,512]{2,1,0:T(8,128)} fusion(f32[5,512,256]{2,1,0:T(8,128)} %get-tuple-element.236, f32[5,512,256]{2,1,0:T(8,128)S(1)} %get-tuple-element.237, f32[5,512,512]{2,1,0:T(8,128)} %get-tuple-element.248, pred[]{:T(512)S(6)} %compare.7), kind=kLoop, calls=%fused_computation.1.clone.1 | loop fusion | flops 3932160 | bytes 15728641 | tf_op jit(solution)/shard_map/while/body/eval_jaxpr/add | solution.py:91
  265.2 7.0 %maximum_add_fusion.2 = f32[5,512,512]{2,1,0:T(8,128)} fusion(f32[5,512,256]{2,1,0:T(8,128)} %get-tuple-element.236, f32[5,512,256]{2,1,0:T(8,128)S(1)} %get-tuple-element.237, f32[5,512,512]{2,1,0:T(8,128)} %get-tuple-element.248, pred[]{:T(512)S(6)} %compare.7), kind=kLoop, calls=%fused_computation.1.clone.1 | loop fusion | flops 3932160 | bytes 15728641 | tf_op jit(solution)/shard_map/while/body/eval_jaxpr/add | solution.py:91
  272.2 11.1 %convolution_bitcast_fusion.1 = f32[5,512,512]{2,1,0:T(8,128)S(1)} fusion(f32[5,512,512]{2,1,0:T(8,128)} %get-tuple-element.143, f32[512]{0:T(512)S(1)} %fusion.68, s32[512]{0:T(512)S(1)} %add_select_fusion.3, f32[512]{0:T(512)S(1)} %fusion.70, pred[512]{0:T(512)(128)(4,1)S(1)} %get-tuple-element.199, pred[512]{0:T(512)(128)(4,1)S(1)} %get-tuple-element.200), kind=kOutput, calls=%fused_computation.12 | convolution fusion | flops 4031512576 | bytes 10492928 | tf_op jit(solution)/shard_map/kcf,ft->ktc/dot_general | solution.py:96
  (92 shorter events, 90.5 us)
Async XLA Ops:
  0.0 24.8 %copy-start = (bf16[3072,512]{1,0:T(8,128)(2,1)S(1)}, bf16[3072,512]{1,0:T(8,128)(2,1)}, u32[]{:S(2)}) copy-start(bf16[3072,512]{1,0:T(8,128)(2,1)} %param.12) | copy-start | bytes 9437188
  0.0 15.8 %copy-start.4 = (bf16[128,4096]{1,0:T(8,128)(2,1)S(1)}, bf16[128,4096]{1,0:T(8,128)(2,1)}, u32[]{:S(2)}) copy-start(bf16[128,4096]{1,0:T(8,128)(2,1)} %param.10) | copy-start | bytes 3145732
  1.0 15.0 %collective-permute-start.1 = (bf16[2,4096]{1,0:T(2,128)(2,1)S(1)}, bf16[2,4096]{1,0:T(2,128)(2,1)S(1)}, u32[]{:S(2)}, u32[]{:S(2)}) collective-permute-start(bf16[2,4096]{1,0:T(2,128)(2,1)S(1)} %slice.114), channel_id=1, source_target_pairs={{0,1},{1,2},{2,3},{3,4},{4,5},{5,6},{6,7},{7,8},{8,9},{9,10},{10,1... | collective-permute-start | bytes 49160 | tf_op jit(solution)/shard_map/ppermute | solution.py:10
  5.5 10.5 %collective-permute-start.2 = (bf16[2,4096]{1,0:T(2,128)(2,1)S(1)}, bf16[2,4096]{1,0:T(2,128)(2,1)S(1)}, u32[]{:S(2)}, u32[]{:S(2)}) collective-permute-start(bf16[2,4096]{1,0:T(2,128)(2,1)S(1)} %slice.120), channel_id=1, source_target_pairs={{0,1},{1,2},{2,3},{3,4},{4,5},{5,6},{6,7},{7,8},{8,9},{9,10},{10,1... | collective-permute-start | bytes 49160 | tf_op jit(solution)/shard_map/ppermute | solution.py:10
  9.9 37.6 %collective-permute-start = (bf16[2,4096]{1,0:T(2,128)(2,1)S(1)}, bf16[2,4096]{1,0:T(2,128)(2,1)S(1)}, u32[]{:S(2)}, u32[]{:S(2)}) collective-permute-start(bf16[2,4096]{1,0:T(2,128)(2,1)S(1)} %slice.107), channel_id=1, source_target_pairs={{0,1},{1,2},{2,3},{3,4},{4,5},{5,6},{6,7},{7,8},{8,9},{9,10},{10,1... | collective-permute-start | bytes 49160 | tf_op jit(solution)/shard_map/ppermute | solution.py:10
  18.6 21.7 %all-to-all-start.1 = ((bf16[128,8,512]{2,0,1:T(8,128)(2,1)}), bf16[128,8,512]{2,0,1:T(8,128)(2,1)}, u32[]{:S(2)}, u32[]{:S(2)}) async-start(bf16[128,8,512]{2,0,1:T(8,128)(2,1)} %bitcast.61), calls=%async_computation.1 | async-start | bytes 2097152 | tf_op jit(solution)/shard_map/all_to_all | solution.py:71
  24.7 1.0 copy-start.2
  40.2 60.8 %collective-permute-start.3 = (bf16[1024,512]{1,0:T(8,128)(2,1)}, bf16[1024,512]{1,0:T(8,128)(2,1)}, u32[]{:S(2)}, u32[]{:S(2)}) collective-permute-start(bf16[1024,512]{1,0:T(8,128)(2,1)} %bitcast.16), channel_id=1, source_target_pairs={{0,24},{8,32},{16,40},{24,48},{32,56},{40,64},{48,72},{56,80},{64,... | collective-permute-start | bytes 3145736 | tf_op jit(solution)/shard_map/ppermute | solution.py:10
  42.1 58.9 %collective-permute-start.4 = (bf16[1024,512]{1,0:T(8,128)(2,1)}, bf16[1024,512]{1,0:T(8,128)(2,1)}, u32[]{:S(2)}, u32[]{:S(2)}) collective-permute-start(bf16[1024,512]{1,0:T(8,128)(2,1)} %bitcast.16), channel_id=1, source_target_pairs={{0,16},{8,24},{16,32},{24,40},{32,48},{40,56},{48,64},{56,72},{64,... | collective-permute-start | bytes 3145736 | tf_op jit(solution)/shard_map/ppermute | solution.py:10
  44.1 57.0 %collective-permute-start.5 = (bf16[1024,512]{1,0:T(8,128)(2,1)}, bf16[1024,512]{1,0:T(8,128)(2,1)}, u32[]{:S(2)}, u32[]{:S(2)}) collective-permute-start(bf16[1024,512]{1,0:T(8,128)(2,1)} %bitcast.16), channel_id=1, source_target_pairs={{0,8},{8,16},{16,24},{24,32},{32,40},{40,48},{48,56},{56,64},{64,7... | collective-permute-start | bytes 3145736 | tf_op jit(solution)/shard_map/ppermute | solution.py:10
  49.2 235.9 %all-to-all-start = ((bf16[128,8,512]{2,0,1:T(8,128)(2,1)}), bf16[128,8,512]{2,0,1:T(8,128)(2,1)}, u32[]{:S(2)}, u32[]{:S(2)}) async-start(bf16[128,8,512]{2,0,1:T(8,128)(2,1)} %bitcast.55), calls=%async_computation | async-start | bytes 2097152 | tf_op jit(solution)/shard_map/all_to_all | solution.py:70
  53.7 49.7 %copy-start.3 = (s32[512,512]{0,1:T(8,128)S(1)}, s32[512,512]{0,1:T(8,128)}, u32[]{:S(2)}) copy-start(s32[512,512]{0,1:T(8,128)} %copy-done.2) | copy-start | bytes 3145732
  283.3 1.8 copy-start.5
  283.4 5.4 %copy-start.1 = (bf16[3072,512]{1,0:T(8,128)(2,1)S(1)}, bf16[3072,512]{1,0:T(8,128)(2,1)}, u32[]{:S(2)}) copy-start(bf16[3072,512]{1,0:T(8,128)(2,1)} %param.12) | copy-start | bytes 9437188
where the time goes:
time: 290 us; the launch traced here: 289 us
  other arithmetic  170 us (59%)
  waiting for transfers between devices  51.7 us (18%)
  matrix products  33.6 us (12%)
  starting transfers between devices  26.2 us (9%)
  local copies, waits for them, and re-layouts  7.1 us (2%)
    add x12, other arithmetic, accumulate(): return totals + packed_product(filter_slice[None], inputs, first_bin)  82.2 us
    sub x12, other arithmetic, packed_product(): filter_real * signal_real - (1.0 - first_bin) * filter_imag * signal_imag  58 us
    ppermute x6, waiting for transfers between devices, passed_along(): return lax.ppermute(block, axis, route)  47.4 us
    dot_general x2, matrix products, spectra(): jnp.einsum('jbc,bf->jcf', blocks, forward, precision=lax.Precision.HIGH)  22.5 us
    mul x12, other arithmetic, packed_product(): (1.0 - first_bin) * filter_imag * signal_imag  16.1 us
    ppermute x6, starting transfers between devices, passed_along(): return lax.ppermute(block, axis, route)  16 us
    dot_general x1, matrix products, local(): jnp.einsum('kcf,ft->ktc', totals, inverse, precision=lax.Precision.HIGH)  11.1 us
  transfers between devices with their start and end apart: 8, of which 2 were waited for; matrix products, arithmetic and copies ran while one was open for 71% of the time, Pallas kernels for 0%

commit v1 on v0

v1 whole, which is shorter than its diff:
```python
import jax
import jax.numpy as jnp
import ml_dtypes
import numpy as np
from jax import lax
from jax.experimental import pallas as pl
from jax.experimental.pallas import tpu as pltpu
from jax.sharding import PartitionSpec as P

MESH = pl.DeviceIdType.MESH
BLOCK = 512
LANES = 128
ROWS = 128
PIECES = 4
GROUPS = 8
PEERS = PIECES * GROUPS
PIECE = ROWS * GROUPS
TAPS = 3072
HALO = TAPS // BLOCK
OWN = PIECES * PIECE // BLOCK
BF16, F32 = jnp.bfloat16, jnp.float32


def tables():
    n, m = np.arange(BLOCK), np.arange(BLOCK)
    phase = ((4 * m[:, None] + 1) * n[None, :]) % (4 * BLOCK)
    angle = 2.0 * np.pi * phase / (4 * BLOCK)
    forward = np.concatenate([np.cos(angle), -np.sin(angle)], axis=0)

    def parts(table):
        high = table.astype(ml_dtypes.bfloat16)
        return high, (table - high.astype(np.float64)).astype(ml_dtypes.bfloat16)

    high, low = parts(forward)
    back_high, back_low = parts(forward.T / BLOCK)
    return np.concatenate([high, low], axis=1), np.stack([back_high, back_low])


def kernel(
    queries,
    keys,
    values,
    short_filter,
    long_filter,
    skip_gain,
    forward_hbm,
    inverse_hbm,
    q_out,
    r_out,
    key_buf,
    value_buf,
    query_buf,
    short_buf,
    filter_buf,
    forward,
    inverse,
    edge_out,
    edge_in,
    edge,
    gated_buf,
    q_buf,
    signal,
    spectra,
    filter_spectra,
    product,
    result,
    load_sem,
    edge_sem,
    gated_send,
    gated_recv,
    halo_send,
    halo_recv,
    q_send,
    q_recv,
    r_send,
    r_recv,
    own_sem,
):
    stretch, grp = lax.axis_index("stretch"), lax.axis_index("grp")
    plane, piece = lax.div(stretch, PIECES), lax.rem(stretch, PIECES)
    half, row = lax.div(grp, 4), lax.rem(grp, 4)

    def peer(step, sign):
        kp, ky, kx = lax.rem(step, 4), lax.rem(lax.div(step, 4), 4), lax.div(step, 16)
        p = lax.rem(piece + sign * kp + 4, 4)
        y = lax.rem(row + sign * ky + 4, 4)
        h = lax.rem(half + kx, 2)
        return p, h * 4 + y

    def place(p, g):
        return HALO + 2 * p + lax.div(g, 4), pl.ds(pl.multiple_of(lax.rem(g, 4) * ROWS, ROWS), ROWS)

    own_lanes = pl.ds(pl.multiple_of(piece * LANES, LANES), LANES)
    loads = [
        pltpu.make_async_copy(keys, key_buf, load_sem.at[0]),
        pltpu.make_async_copy(values, value_buf, load_sem.at[1]),
        pltpu.make_async_copy(queries, query_buf, load_sem.at[2]),
        pltpu.make_async_copy(short_filter, short_buf, load_sem.at[3]),
        pltpu.make_async_copy(long_filter.at[:, :, own_lanes], filter_buf, load_sem.at[4]),
        pltpu.make_async_copy(forward_hbm, forward, load_sem.at[5]),
        pltpu.make_async_copy(inverse_hbm, inverse, load_sem.at[6]),
    ]
    for load in loads:
        load.start()

    barrier = pltpu.get_barrier_semaphore()

    def greet(step, carry):
        p, g = peer(step, 1)
        pl.semaphore_signal(barrier, inc=1, device_id=(plane * PIECES + p, g), device_id_type=MESH)
        return carry

    lax.fori_loop(1, PEERS, greet, 0)
    has_before, has_after = plane > 0, plane < 3
    corner = jnp.logical_and(piece == PIECES - 1, grp == GROUPS - 1)

    @pl.when(has_before)
    def _():
        pl.semaphore_signal(barrier, inc=1, device_id=(stretch - PIECES, grp), device_id_type=MESH)

    @pl.when(jnp.logical_and(has_before, jnp.logical_and(piece == 0, grp == 0)))
    def _():
        pl.semaphore_signal(barrier, inc=1, device_id=(stretch - 1, GROUPS - 1), device_id_type=MESH)

    @pl.when(jnp.logical_not(has_before))
    def _():
        signal[:HALO] = jnp.zeros((HALO, BLOCK, LANES), BF16)

    for load in loads[:4]:
        load.wait()
    fold = 512
    row_at = lax.broadcasted_iota(jnp.int32, (16, fold), 0)
    for n, buf in enumerate((key_buf, value_buf, query_buf)):
        tail = buf[ROWS - 16 :, :].astype(F32)
        packed = jnp.zeros((16, fold), F32)
        for r in range(2):
            for e in range(8):
                part = tail[14 + r : 15 + r, e * fold : (e + 1) * fold]
                packed = jnp.where(row_at == r * 8 + e, part, packed)
        edge_out[n] = packed.astype(BF16)

    after = has_after.astype(jnp.int32)
    pl.semaphore_wait(barrier, PEERS - 1 + after + after * corner.astype(jnp.int32))

    wraps = grp == GROUPS - 1
    next_device = (
        jnp.where(wraps, lax.rem(stretch + 1, 16), stretch),
        jnp.where(wraps, 0, grp + 1),
    )
    edge_copy = pltpu.make_async_remote_copy(
        edge_out, edge_in, edge_sem.at[0], edge_sem.at[1], device_id=next_device, device_id_type=MESH
    )
    is_first = jnp.logical_and(stretch == 0, grp == 0)
    is_last = jnp.logical_and(stretch == 15, wraps)

    @pl.when(jnp.logical_not(is_last))
    def _():
        edge_copy.start()

    @pl.when(is_first)
    def _():
        edge_in[...] = jnp.zeros_like(edge_in)

    @pl.when(jnp.logical_not(is_first))
    def _():
        edge_copy.wait_recv()

    for n in range(3):
        packed = edge_in[n].astype(F32)
        for r in range(2):
            for e in range(8):
                edge[n, r : r + 1, e * fold : (e + 1) * fold] = packed[r * 8 + e : r * 8 + e + 1]

    at = lax.broadcasted_iota(jnp.int32, (ROWS, LANES), 0)

    def shorten(buf, n, position, block):
        lanes = pl.ds(pl.multiple_of(block * LANES, LANES), LANES)
        now = buf[:, lanes].astype(F32)
        two, one = edge[n, 0:1, lanes], edge[n, 1:2, lanes]
        back1 = jnp.where(at == 0, one, pltpu.roll(now, 1, 0))
        back2 = jnp.where(at == 0, two, jnp.where(at == 1, one, pltpu.roll(now, 2, 0)))
        taps = [short_buf[tap, position : position + 1, lanes] for tap in range(3)]
        return taps[0] * now + taps[1] * back1 + taps[2] * back2

    def gated_copy(step):
        p, g = peer(step, 1)
        block, rows = place(piece, grp)
        return pltpu.make_async_remote_copy(
            gated_buf.at[step],
            signal.at[block, rows],
            gated_send.at[step],
            gated_recv.at[step],
            device_id=(plane * PIECES + p, g),
            device_id_type=MESH,
        )

    def make_gated(step):
        p, g = peer(step, 1)
        block = g * PIECES + p
        gated_buf[step] = (shorten(key_buf, 0, 1, block) * shorten(value_buf, 1, 2, block)).astype(BF16)

    def send_gated(step, carry):
        make_gated(step)
        gated_copy(step).start()
        return carry

    lax.fori_loop(1, PEERS, send_gated, 0)
    make_gated(0)
    own_block, own_rows = place(piece, grp)
    own_gated = pltpu.make_async_copy(gated_buf.at[0], signal.at[own_block, own_rows], gated_recv.at[0])
    own_gated.start()

    def halo_copy(step):
        p, g = peer(step, -1)
        block, rows = place(p, g)
        return pltpu.make_async_remote_copy(
            signal.at[block, rows],
            signal.at[block - OWN, rows],
            halo_send.at[step],
            halo_recv.at[p],
            device_id=(lax.rem(stretch + PIECES, 16), grp),
            device_id_type=MESH,
        )

    def pass_on(step):
        p, _ = peer(step, -1)

        @pl.when(jnp.logical_and(has_after, p > 0))
        def _():
            halo_copy(step).start()

    def transform(source, block, target, rows):
        pair = jnp.concatenate([source[block], source[block + 1]], axis=1)
        bins = jnp.dot(forward[rows, :], jnp.concatenate([pair, pair], axis=0), preferred_element_type=F32)
        target[block, rows] = bins[:, :LANES]
        target[block + 1, rows] = bins[:, LANES:]

    def shorten_q(block):
        lanes = pl.ds(pl.multiple_of(block * LANES, LANES), LANES)
        q_buf[:, lanes] = shorten(query_buf, 2, 0, block).astype(BF16)

    own_gated.wait()
    pass_on(0)
    shorten_q(0)
    for load in loads[4:]:
        load.wait()

    def receive(step, carry):
        shorten_q(step)

        @pl.when(lax.rem(step, 5) == 0)
        def _():
            unit = lax.div(step, 5) - 1
            half_rows = pl.ds(pl.multiple_of(lax.rem(unit, 2) * BLOCK, BLOCK), BLOCK)
            transform(filter_buf, 2 * lax.div(unit, 2), filter_spectra, half_rows)

        gated_copy(step).wait_recv()
        pass_on(step)
        return carry

    lax.fori_loop(1, PEERS, receive, 0)

    def q_copy(step):
        other = lax.rem(grp + step, GROUPS)
        return pltpu.make_async_remote_copy(
            q_buf.at[:, pl.ds(pl.multiple_of(other * 512, 512), 512)],
            q_out.at[pl.ds(pl.multiple_of(grp * ROWS, ROWS), ROWS)],
            q_send.at[step],
            q_recv.at[step],
            device_id=(stretch, other),
            device_id_type=MESH,
        )

    own_q = pltpu.make_async_copy(
        q_buf.at[:, pl.ds(pl.multiple_of(grp * 512, 512), 512)],
        q_out.at[pl.ds(pl.multiple_of(grp * ROWS, ROWS), ROWS)],
        own_sem.at[0],
    )
    own_q.start()
    for step in range(1, GROUPS):
        q_copy(step).start()

    def transform_signal(first, count):
        def body(unit, carry):
            half_rows = pl.ds(pl.multiple_of(lax.rem(unit, 2) * BLOCK, BLOCK), BLOCK)
            transform(signal, first + 2 * lax.div(unit, 2), spectra, half_rows)
            return carry

        lax.fori_loop(0, count, body, 0)

    gain = skip_gain[own_lanes].reshape(1, LANES)

    def convolve(p):
        def bins(tile, carry):
            real = pl.ds(pl.multiple_of(tile * 16, 16), 16)
            imag = pl.ds(pl.multiple_of(BLOCK + tile * 16, 16), 16)
            window = []
            for b in range(HALO + 1):
                here, before = 2 * p + 1 + b, 2 * p + b
                window.append(
                    (
                        spectra[here, real] - spectra[before, imag],
                        spectra[here, imag] + spectra[before, real],
                    )
                )
            sums = [None, None]
            for i in range(HALO):
                fr, fi = filter_spectra[i, real], filter_spectra[i, imag]
                for o in range(2):
                    sr, si = window[HALO - 1 + o - i]
                    re, im = fr * sr - fi * si, fr * si + fi * sr
                    sums[o] = (re, im) if sums[o] is None else (sums[o][0] + re, sums[o][1] + im)
            for at_rows, n in ((real, 0), (imag, 1)):
                both = jnp.concatenate([sums[0][n], sums[1][n]], axis=1)
                high = both.astype(BF16)
                product[0, at_rows] = high
                product[1, at_rows] = (both - high.astype(F32)).astype(BF16)
            return carry

        lax.fori_loop(0, BLOCK // 16, bins, 0)
        back = (
            jnp.dot(inverse[0], product[0], preferred_element_type=F32)
            + jnp.dot(inverse[0], product[1], preferred_element_type=F32)
            + jnp.dot(inverse[1], product[0], preferred_element_type=F32)
        )
        for o in range(2):
            direct = gain * signal[HALO + 2 * p + o].astype(F32)
            result[p, pl.ds(o * BLOCK, BLOCK)] = (back[:, o * LANES : (o + 1) * LANES] + direct).astype(BF16)

    def r_copy(p):
        return pltpu.make_async_remote_copy(
            result.at[p],
            r_out.at[:, own_lanes],
            r_send.at[p],
            r_recv.at[piece],
            device_id=(plane * PIECES + p, grp),
            device_id_type=MESH,
        )

    own_r = pltpu.make_async_copy(result.at[piece], r_out.at[:, own_lanes], own_sem.at[1])

    def send_result(p):
        @pl.when(piece != p)
        def _():
            r_copy(p).start()

        @pl.when(piece == p)
        def _():
            own_r.start()

    transform_signal(HALO, 2 * PIECES)
    convolve(3)
    send_result(3)
    for p in (2, 1, 0):

        @pl.when(has_before)
        def _(p=p):
            blocks = signal.at[pl.ds(2 * p, 2)]
            pltpu.make_async_copy(blocks, blocks, halo_recv.at[p + 1]).wait()

        transform_signal(2 * p, 2)
        convolve(p)
        send_result(p)

    own_q.wait()
    for step in range(1, GROUPS):
        q_copy(step).wait()
    own_r.wait()
    for p in range(PIECES):

        @pl.when(piece != p)
        def _(p=p):
            r_copy(p).wait_send()
            lanes = pl.ds(p * LANES, LANES)
            pltpu.make_async_copy(r_out.at[:, lanes], r_out.at[:, lanes], r_recv.at[p]).wait()

    @pl.when(jnp.logical_not(is_last))
    def _():
        edge_copy.wait_send()

    def sent(step, carry):
        gated_copy(step).wait_send()
        return carry

    lax.fori_loop(1, PEERS, sent, 0)

    def halo_sent(step, carry):
        p, _ = peer(step, -1)

        @pl.when(jnp.logical_and(has_after, p > 0))
        def _():
            halo_copy(step).wait_send()

        return carry

    lax.fori_loop(0, PEERS, halo_sent, 0)


def local(queries, keys, values, short_filter, long_filter, skip_gain):
    width = queries.shape[1]
    slice_width = width // GROUPS
    forward, inverse = tables()
    hbm, vmem = pl.BlockSpec(memory_space=pl.ANY), pl.BlockSpec(memory_space=pltpu.VMEM)
    dma = pltpu.SemaphoreType.DMA
    q_slices, convolved = pl.pallas_call(
        kernel,
        out_shape=[jax.ShapeDtypeStruct((PIECE, slice_width), BF16)] * 2,
        in_specs=[hbm, hbm, hbm, hbm, hbm, vmem, hbm, hbm],
        out_specs=[hbm, hbm],
        scratch_shapes=[
            pltpu.VMEM((ROWS, width), BF16),
            pltpu.VMEM((ROWS, width), BF16),
            pltpu.VMEM((ROWS, width), BF16),
            pltpu.VMEM((3, 3, width), F32),
            pltpu.VMEM((HALO, BLOCK, LANES), BF16),
            pltpu.VMEM(forward.shape, BF16),
            pltpu.VMEM(inverse.shape, BF16),
            pltpu.VMEM((3, 16, 512), BF16),
            pltpu.VMEM((3, 16, 512), BF16),
            pltpu.VMEM((3, 8, width), F32),
            pltpu.VMEM((PEERS, ROWS, LANES), BF16),
            pltpu.VMEM((ROWS, width), BF16),
            pltpu.VMEM((HALO + OWN, BLOCK, LANES), BF16),
            pltpu.VMEM((HALO + OWN, 2 * BLOCK, LANES), F32),
            pltpu.VMEM((HALO, 2 * BLOCK, LANES), F32),
            pltpu.VMEM((2, 2 * BLOCK, 2 * LANES), BF16),
            pltpu.VMEM((PIECES, PIECE, LANES), BF16),
            dma((7,)),
            dma((2,)),
            dma((PEERS,)),
            dma((PEERS,)),
            dma((PEERS,)),
            dma((PIECES,)),
            dma((GROUPS,)),
            dma((GROUPS,)),
            dma((PIECES,)),
            dma((PIECES,)),
            dma((2,)),
        ],
        compiler_params=pltpu.CompilerParams(
            collective_id=0, has_side_effects=True, vmem_limit_bytes=56 * 2**20
        ),
        cost_estimate=pl.CostEstimate(flops=9 * 10**9, bytes_accessed=16 * 2**20, transcendentals=0),
    )(
        queries,
        keys,
        values,
        short_filter,
        long_filter.reshape(HALO, BLOCK, slice_width),
        skip_gain,
        jnp.asarray(forward),
        jnp.asarray(inverse),
    )
    return (q_slices.astype(F32) * convolved.astype(F32)).astype(BF16)


def solution(mesh):
    return jax.shard_map(
        local,
        mesh=mesh,
        in_specs=(
            P(("stretch", "grp"), None),
            P(("stretch", "grp"), None),
            P(("stretch", "grp"), None),
            P(),
            P(None, "grp"),
            P("grp"),
        ),
        out_specs=P("stretch", "grp"),
        check_vma=False,
    )
```

time: 290 us -> 60 us (0.21)
  other arithmetic: 170 us -> 2.8 us
  Pallas kernels: 0 us -> 57.1 us
  waiting for transfers between devices: 51.7 us -> 0 us
  matrix products: 33.6 us -> 0 us
  starting transfers between devices: 26.2 us -> 0 us
  local copies, waits for them, and re-layouts: 7.1 us -> 0 us
    add x13 -> x0, other arithmetic: 84 us -> none  [the longest x12 82.2 us: accumulate(): return totals + packed_product(filter_slice[None], inputs, first_bin)]
    sub x24 -> x0, other arithmetic: 58 us -> none  [the longest x12 58 us: packed_product(): filter_real * signal_real - (1.0 - first_bin) * filter_imag * signal_imag]
    pallas_call x0 -> x1, Pallas kernels: none -> 57.1 us  [local(): pl.pallas_call(kernel, out_shape=[jax.ShapeDtypeStruct((PIECE, slice_widt...]
    ppermute x6 -> x0, waiting for transfers between devices: 47.4 us -> none  [passed_along(): return lax.ppermute(block, axis, route)]
    dot_general x3 -> x0, matrix products: 33.6 us -> none  [the longest x2 22.5 us: spectra(): jnp.einsum('jbc,bf->jcf', blocks, forward, precision=lax.Precision.HIGH)]
    mul x12 -> x0, other arithmetic: 16.1 us -> none  [packed_product(): (1.0 - first_bin) * filter_imag * signal_imag]
    ppermute x6 -> x0, starting transfers between devices: 16 us -> none  [passed_along(): return lax.ppermute(block, axis, route)]
    all_to_all x2 -> x0, starting transfers between devices: 10.1 us -> none  [the longest x1 5.69 us: local(): lax.all_to_all(gated, 'grp', split_axis=1, concat_axis=0, tiled=True)]
  transfers between devices with their start and end apart: 8 -> 0, of which waited for: 2 -> 0; matrix products, arithmetic and copies ran while one was open for 71% -> 0% of each run, Pallas kernels for 0% -> 0%
where the time goes in v1:
time: 60 us; the launch traced here: 59.9 us
  Pallas kernels  57.1 us (95%)
  other arithmetic  2.8 us (5%)
    pallas_call x1, Pallas kernels, local(): pl.pallas_call(kernel, out_shape=[jax.ShapeDtypeStruct((PIECE, slice_widt...  57.1 us
    convert_element_type x1, other arithmetic, local(): return (q_slices.astype(F32) * convolved.astype(F32)).astype(BF16)  2.8 us

profile of v1, /device:TPU:96, one launch (start us, length us, event | category | flops | bytes accessed | tf_op | source)
XLA Modules:
  0.0 59.9 jit_solution(1506851600746690546)
XLA Ops:
  0.0 57.1 %shard_map.82 = (bf16[1024,512]{1,0:T(8,128)(2,1)}, bf16[1024,512]{1,0:T(8,128)(2,1)}) custom-call(bf16[128,4096]{1,0:T(8,128)(2,1)} %queries.1, bf16[128,4096]{1,0:T(8,128)(2,1)} %keys.1, bf16[128,4096]{1,0:T(8,128)(2,1)} %values.1, f32[3,3,4096]{2,1,0:T(4,128)} %short_filter.1, bf16[6,512,512]{2,1,0:T(8,128)(2,1)} %bitcast.1, f32[512]{0:T(512)} %skip_gain.1, ...), custom_call_target="tpu_custom_call" | custom-call | flops 8999999488 | bytes 16777216 | tf_op jit(solution)/shard_map/pallas_call | solution.py:405
  57.1 2.8 %multiply_convert_fusion = bf16[1024,512]{1,0:T(8,128)(2,1)} fusion(bf16[1024,512]{1,0:T(8,128)(2,1)} %get-tuple-element.8, bf16[1024,512]{1,0:T(8,128)(2,1)} %get-tuple-element.7), kind=kLoop, calls=%fused_computation | loop fusion | flops 2097152 | bytes 3145728 | tf_op jit(solution)/shard_map/convert_element_type | solution.py:454

commit v2 on v1

v2 whole, which is shorter than its diff:
```python
import jax
import jax.numpy as jnp
import ml_dtypes
import numpy as np
from jax import lax
from jax.experimental import pallas as pl
from jax.experimental.pallas import tpu as pltpu
from jax.sharding import PartitionSpec as P

MESH = pl.DeviceIdType.MESH
BLOCK = 512
LANES = 128
ROWS = 128
HEAD = 16
PIECES = 4
GROUPS = 8
PEERS = PIECES * GROUPS
PIECE = ROWS * GROUPS
TAPS = 3072
HALO = TAPS // BLOCK
OWN = PIECES * PIECE // BLOCK
HALO_PIECES = TAPS // PIECE
AHEAD = 16
PROMPT = 2
BF16, F32 = jnp.bfloat16, jnp.float32
Q_STEPS = (4, 6, 5, 7, 1, 3, 2)
ORDER = (
    ("piece", 3),
    ("halo", 2),
    ("halo", 1),
    ("piece", 1),
    ("piece", 2),
    ("halo", 0),
    ("piece", 0),
)
VMEM_LIMIT = 56 * 2**20


def tables():
    n, m = np.arange(BLOCK), np.arange(BLOCK)
    phase = ((4 * m[:, None] + 1) * n[None, :]) % (4 * BLOCK)
    angle = 2.0 * np.pi * phase / (4 * BLOCK)
    forward = np.concatenate([np.cos(angle), -np.sin(angle)], axis=0)

    def parts(table):
        high = table.astype(ml_dtypes.bfloat16)
        return high, (table - high.astype(np.float64)).astype(ml_dtypes.bfloat16)

    high, low = parts(forward)
    back_high, back_low = parts(forward.T / BLOCK)
    return np.concatenate([high, low], axis=1), np.concatenate([back_high, back_high, back_low], axis=1)


def kernel(
    queries,
    keys,
    values,
    short_filter,
    long_filter,
    skip_gain,
    forward_hbm,
    inverse_hbm,
    q_out,
    r_out,
    key_buf,
    value_buf,
    short_buf,
    filter_buf,
    forward,
    inverse,
    edge_out,
    edge_in,
    edge,
    gated_buf,
    head_buf,
    heads,
    q_raw,
    q_buf,
    signal,
    spectra,
    filter_spectra,
    product,
    result,
    load_sem,
    edge_sem,
    plane_sem,
    gated_send,
    gated_recv,
    head_send,
    head_recv,
    halo_send,
    halo_recv,
    halo_head_send,
    halo_head_recv,
    q_send,
    q_recv,
    q_edge_sem,
    r_send,
    r_recv,
    own_sem,
):
    stretch, grp = lax.axis_index("stretch"), lax.axis_index("grp")
    plane, piece = lax.div(stretch, PIECES), lax.rem(stretch, PIECES)
    half, row = lax.div(grp, 4), lax.rem(grp, 4)
    has_before, has_after = plane > 0, plane < 3
    group_ends = grp == GROUPS - 1
    is_first = jnp.logical_and(stretch == 0, grp == 0)
    is_last = jnp.logical_and(stretch == 15, group_ends)
    next_stretch = lax.rem(stretch + 1, 16)

    def peer(step, sign):
        kp, ky, kx = lax.rem(step, 4), lax.rem(lax.div(step, 4), 4), lax.div(step, 16)
        p = lax.rem(piece + sign * kp + 4, 4)
        y = lax.rem(row + sign * ky + 4, 4)
        h = lax.rem(half + kx, 2)
        return p, h * 4 + y

    def aligned(index, size):
        return pl.ds(pl.multiple_of(index * size, size), size)

    def place(p, g):
        return HALO + 2 * p + lax.div(g, 4), aligned(lax.rem(g, 4), ROWS)

    own_lanes = aligned(piece, LANES)
    loads = [
        pltpu.make_async_copy(keys, key_buf, load_sem.at[0]),
        pltpu.make_async_copy(values, value_buf, load_sem.at[1]),
        pltpu.make_async_copy(short_filter, short_buf, load_sem.at[2]),
        pltpu.make_async_copy(long_filter.at[:, :, own_lanes], filter_buf, load_sem.at[3]),
        pltpu.make_async_copy(forward_hbm, forward, load_sem.at[4]),
        pltpu.make_async_copy(inverse_hbm, inverse, load_sem.at[5]),
    ]
    for load in loads[:5]:
        load.start()

    barrier = pltpu.get_barrier_semaphore()

    def tell(s, g):
        pl.semaphore_signal(barrier, inc=1, device_id=(s, g), device_id_type=MESH)

    for d in range(1, GROUPS):
        tell(stretch, lax.rem(grp + d, GROUPS))
    pieces = [plane * PIECES + lax.rem(piece + d, PIECES) for d in range(1, PIECES)]
    for s in pieces:
        tell(s, grp)

    @pl.when(has_before)
    def _():
        tell(stretch - PIECES, grp)

    @pl.when(jnp.logical_and(has_before, piece == 0))
    def _():
        tell(stretch - 1, grp)

    @pl.when(jnp.logical_and(grp == 0, jnp.logical_not(is_first)))
    def _():
        tell(stretch - 1, GROUPS - 1)

    @pl.when(jnp.logical_not(has_before))
    def _():
        signal[:HALO] = jnp.zeros((HALO, BLOCK, LANES), BF16)

    for load in loads[:3]:
        load.wait()
    fold = 512
    row_at = lax.broadcasted_iota(jnp.int32, (16, fold), 0)
    for n, buf in enumerate((key_buf, value_buf)):
        tail = buf[ROWS - 16 :, :].astype(F32)
        packed = jnp.zeros((16, fold), F32)
        for r in range(2):
            for e in range(8):
                part = tail[14 + r : 15 + r, e * fold : (e + 1) * fold]
                packed = jnp.where(row_at == r * 8 + e, part, packed)
        edge_out[n] = packed.astype(BF16)

    def shorten(now, two, one, position, block):
        at = lax.broadcasted_iota(jnp.int32, now.shape, 0)
        back1 = jnp.where(at == 0, one, pltpu.roll(now, 1, 0))
        back2 = jnp.where(at == 0, two, jnp.where(at == 1, one, pltpu.roll(now, 2, 0)))
        lanes = aligned(block, LANES)
        taps = [short_buf[tap, position : position + 1, lanes] for tap in range(3)]
        return taps[0] * now + taps[1] * back1 + taps[2] * back2

    def block_of(step):
        p, g = peer(step, 1)
        return g * PIECES + p

    def gate_first(step):
        block = block_of(step)
        lanes = aligned(block, LANES)
        factors = [
            shorten(buf[:HEAD, lanes].astype(F32), edge[n, 0:1, lanes], edge[n, 1:2, lanes], n + 1, block)
            for n, buf in enumerate((key_buf, value_buf))
        ]
        head_buf[step] = (factors[0] * factors[1]).astype(BF16)

    def gate_rest(step):
        block = block_of(step)
        lanes = aligned(block, LANES)
        factors = []
        for n, buf in enumerate((key_buf, value_buf)):
            now = buf[:, lanes].astype(F32)
            taps = [short_buf[tap, n + 1 : n + 2, lanes] for tap in range(3)]
            factors.append(taps[0] * now + taps[1] * pltpu.roll(now, 1, 0) + taps[2] * pltpu.roll(now, 2, 0))
        gated_buf[step] = (factors[0] * factors[1])[HEAD:].astype(BF16)

    def gate_ahead(step, carry):
        gate_rest(step)
        return carry

    lax.fori_loop(0, AHEAD, gate_ahead, 0)

    def count(flag):
        return flag.astype(jnp.int32)

    pl.semaphore_wait(
        barrier,
        GROUPS - 1 + PIECES - 1
        + count(has_after)
        + count(jnp.logical_and(has_after, piece == PIECES - 1))
        + count(jnp.logical_and(group_ends, jnp.logical_not(is_last))),
    )
    for s in pieces:
        pl.semaphore_signal(plane_sem, inc=1, device_id=(s, grp), device_id_type=MESH)

    edge_copy = pltpu.make_async_remote_copy(
        edge_out,
        edge_in,
        edge_sem.at[0],
        edge_sem.at[1],
        device_id=(jnp.where(group_ends, next_stretch, stretch), jnp.where(group_ends, 0, grp + 1)),
        device_id_type=MESH,
    )

    @pl.when(jnp.logical_not(is_last))
    def _():
        edge_copy.start()

    def rest_of(p, g):
        block, rows = place(p, g)
        return signal.at[block, pl.ds(pl.multiple_of(rows.start + HEAD, HEAD), ROWS - HEAD)]

    def gated_copy(step):
        p, g = peer(step, 1)
        return pltpu.make_async_remote_copy(
            gated_buf.at[step],
            rest_of(piece, grp),
            gated_send.at[step],
            gated_recv.at[step],
            device_id=(plane * PIECES + p, g),
            device_id_type=MESH,
        )

    def head_copy(step):
        p, g = peer(step, 1)
        return pltpu.make_async_remote_copy(
            head_buf.at[step],
            heads.at[HALO_PIECES + piece, grp],
            head_send.at[step],
            head_recv.at[piece],
            device_id=(plane * PIECES + p, g),
            device_id_type=MESH,
        )

    own_rest = pltpu.make_async_copy(gated_buf.at[0], rest_of(piece, grp), gated_recv.at[0])
    own_rest.start()
    pl.semaphore_wait(plane_sem, PIECES - 1)

    def send_rest(step, carry):
        @pl.when(step >= AHEAD)
        def _():
            gate_rest(step)

        gated_copy(step).start()
        return carry

    lax.fori_loop(1, PEERS, send_rest, 0)

    def q_copy(step):
        other = lax.rem(half + step // 4, 2) * 4 + lax.rem(row + step % 4, 4)
        return pltpu.make_async_remote_copy(
            queries.at[:, aligned(other, 512)],
            q_raw.at[pl.ds(pl.multiple_of(16 + grp * ROWS, 16), ROWS)],
            q_send.at[step],
            q_recv.at[step],
            device_id=(stretch, other),
            device_id_type=MESH,
        )

    own_q = pltpu.make_async_copy(
        queries.at[:, aligned(grp, 512)],
        q_raw.at[pl.ds(pl.multiple_of(16 + grp * ROWS, 16), ROWS)],
        own_sem.at[0],
    )
    own_q.start()

    def transform(source, block, target, rows):
        pair = jnp.concatenate([source[block], source[block + 1]], axis=1)
        bins = jnp.dot(forward[rows, :], jnp.concatenate([pair, pair], axis=0), preferred_element_type=F32)
        target[block, rows] = bins[:, :LANES]
        target[block + 1, rows] = bins[:, LANES:]

    def transform_blocks(source, target, first, pairs):
        def body(unit, carry):
            transform(source, first + 2 * lax.div(unit, 2), target, aligned(lax.rem(unit, 2), BLOCK))
            return carry

        lax.fori_loop(0, 2 * pairs, body, 0)

    @pl.when(is_first)
    def _():
        edge_in[...] = jnp.zeros_like(edge_in)

    @pl.when(jnp.logical_not(is_first))
    def _():
        edge_copy.wait_recv()

    for n in range(2):
        packed = edge_in[n].astype(F32)
        for r in range(2):
            for e in range(8):
                edge[n, r : r + 1, e * fold : (e + 1) * fold] = packed[r * 8 + e : r * 8 + e + 1]

    def send_head(step, carry):
        gate_first(step)
        head_copy(step).start()
        return carry

    lax.fori_loop(1, PEERS, send_head, 0)
    gate_first(0)
    own_head = pltpu.make_async_copy(head_buf.at[0], heads.at[HALO_PIECES + piece, grp], head_recv.at[piece])
    own_head.start()
    loads[5].start()

    def halo_copy(p, g):
        block, rows = place(p, g)
        rest = pl.ds(pl.multiple_of(rows.start + HEAD, HEAD), ROWS - HEAD)
        return pltpu.make_async_remote_copy(
            signal.at[block, rest],
            signal.at[block - OWN, rest],
            halo_send.at[p, g],
            halo_recv.at[p],
            device_id=(lax.rem(stretch + PIECES, 16), grp),
            device_id_type=MESH,
        )

    def halo_head_copy(p):
        return pltpu.make_async_remote_copy(
            heads.at[HALO_PIECES + p],
            heads.at[p - 1],
            halo_head_send.at[p],
            halo_head_recv.at[p],
            device_id=(lax.rem(stretch + PIECES, 16), grp),
            device_id_type=MESH,
        )

    def receive(turn, carry):
        for p in (3, 2, 1, 0):
            step = 4 * turn + lax.rem(piece - p + 4, 4)
            _, g = peer(step, -1)
            rest = rest_of(p, g)
            pltpu.make_async_copy(rest, rest, gated_recv.at[step]).wait()
            if p >= PROMPT:

                @pl.when(has_after)
                def _():
                    halo_copy(p, g).start()

        return carry

    def settle(index, target):
        for c in range(GROUPS):
            signal[target + c // 4, (c % 4) * ROWS : (c % 4) * ROWS + HEAD] = heads[index, c]

    loads[3].wait()
    loads[4].wait()
    transform_blocks(filter_buf, filter_spectra, 0, HALO // 2)

    lax.fori_loop(0, GROUPS, receive, 0)
    for p in (3, 2, 1, 0):
        own_heads = heads.at[HALO_PIECES + p]
        pltpu.make_async_copy(own_heads, own_heads, head_recv.at[p]).wait()
        if p > 0:

            @pl.when(has_after)
            def _(p=p):
                halo_head_copy(p).start()
                if p < PROMPT:
                    for g in range(GROUPS):
                        halo_copy(p, g).start()

    for step in Q_STEPS:
        q_copy(step).start()
    for p in (3, 2, 1, 0):
        settle(HALO_PIECES + p, HALO + 2 * p)
    transform_blocks(signal, spectra, HALO, PIECES)

    gain = skip_gain[own_lanes].reshape(1, LANES)

    def convolve(p):
        def bins(tile, carry):
            real, imag = aligned(tile, 16), pl.ds(pl.multiple_of(BLOCK + tile * 16, 16), 16)
            window = []
            for b in range(HALO + 1):
                here, before = 2 * p + 1 + b, 2 * p + b
                window.append(
                    (
                        spectra[here, real] - spectra[before, imag],
                        spectra[here, imag] + spectra[before, real],
                    )
                )
            sums = [None, None]
            for i in range(HALO):
                fr, fi = filter_spectra[i, real], filter_spectra[i, imag]
                for o in range(2):
                    sr, si = window[HALO - 1 + o - i]
                    re, im = fr * sr - fi * si, fr * si + fi * sr
                    sums[o] = (re, im) if sums[o] is None else (sums[o][0] + re, sums[o][1] + im)
            for n, at_rows in ((0, real), (1, imag)):
                both = jnp.concatenate([sums[0][n], sums[1][n]], axis=1)
                high = both.astype(BF16)
                product[0, at_rows] = high
                product[1, at_rows] = (both - high.astype(F32)).astype(BF16)
            return carry

        lax.fori_loop(0, BLOCK // 16, bins, 0)
        high, low = product[0], product[1]
        back = jnp.dot(inverse[...], jnp.concatenate([high, low, high], axis=0), preferred_element_type=F32)
        for o in range(2):
            direct = gain * signal[HALO + 2 * p + o].astype(F32)
            result[p, pl.ds(o * BLOCK, BLOCK)] = (back[:, o * LANES : (o + 1) * LANES] + direct).astype(BF16)

    def r_copy(p):
        return pltpu.make_async_remote_copy(
            result.at[p],
            r_out.at[:, own_lanes],
            r_send.at[p],
            r_recv.at[piece],
            device_id=(plane * PIECES + p, grp),
            device_id_type=MESH,
        )

    own_r = pltpu.make_async_copy(result.at[piece], r_out.at[:, own_lanes], own_sem.at[1])

    def send_result(p):
        @pl.when(piece != p)
        def _():
            r_copy(p).start()

        @pl.when(piece == p)
        def _():
            own_r.start()

    def halo(p):
        @pl.when(has_before)
        def _():
            rests = signal.at[pl.ds(2 * p, 2), pl.ds(0, 4 * (ROWS - HEAD))]
            pltpu.make_async_copy(rests, rests, halo_recv.at[p + 1]).wait()
            pltpu.make_async_copy(heads.at[p], heads.at[p], halo_head_recv.at[p + 1]).wait()
            settle(p, 2 * p)

        transform_blocks(signal, spectra, 2 * p, 1)

    loads[5].wait()
    for what, p in ORDER:
        if what == "halo":
            halo(p)
        else:
            convolve(p)
            send_result(p)

    own_q.wait()
    for step in range(1, GROUPS):
        q_copy(step).wait_recv()
    q_edge = pltpu.make_async_remote_copy(
        q_raw.at[pl.ds(PIECE, 16)],
        q_raw.at[pl.ds(0, 16)],
        q_edge_sem.at[0],
        q_edge_sem.at[1],
        device_id=(next_stretch, grp),
        device_id_type=MESH,
    )

    @pl.when(stretch < 15)
    def _():
        q_edge.start()

    @pl.when(stretch == 0)
    def _():
        q_raw[:16] = jnp.zeros((16, 512), BF16)

    @pl.when(stretch > 0)
    def _():
        q_edge.wait_recv()

    def shorten_q(unit, carry):
        chunk, part = lax.div(unit, 4), lax.rem(unit, 4)
        lanes = aligned(part, LANES)
        now = q_raw[pl.ds(pl.multiple_of(16 + chunk * ROWS, 16), ROWS), lanes].astype(F32)
        tail = q_raw[aligned(chunk, ROWS), lanes][:16].astype(F32)
        q_buf[aligned(chunk, ROWS), lanes] = shorten(
            now, tail[14:15], tail[15:16], 0, grp * 4 + part
        ).astype(BF16)
        return carry

    lax.fori_loop(0, 32, shorten_q, 0)
    q_copy_out = pltpu.make_async_copy(q_buf, q_out, own_sem.at[0])
    q_copy_out.start()

    q_copy_out.wait()
    own_r.wait()
    for p in range(PIECES):

        @pl.when(piece != p)
        def _(p=p):
            r_copy(p).wait_send()
            lanes = pl.ds(p * LANES, LANES)
            pltpu.make_async_copy(r_out.at[:, lanes], r_out.at[:, lanes], r_recv.at[p]).wait()

    for step in range(1, GROUPS):
        q_copy(step).wait_send()

    @pl.when(stretch < 15)
    def _():
        q_edge.wait_send()

    @pl.when(jnp.logical_not(is_last))
    def _():
        edge_copy.wait_send()

    def sent(step, carry):
        gated_copy(step).wait_send()
        head_copy(step).wait_send()
        return carry

    lax.fori_loop(1, PEERS, sent, 0)

    @pl.when(has_after)
    def _():
        for p in range(1, PIECES):
            halo_head_copy(p).wait_send()

            def halo_sent(g, carry, p=p):
                halo_copy(p, g).wait_send()
                return carry

            lax.fori_loop(0, GROUPS, halo_sent, 0)


def local(queries, keys, values, short_filter, long_filter, skip_gain):
    width = queries.shape[1]
    slice_width = width // GROUPS
    forward, inverse = tables()
    hbm, vmem = pl.BlockSpec(memory_space=pltpu.HBM), pl.BlockSpec(memory_space=pltpu.VMEM)
    anywhere = pl.BlockSpec(memory_space=pl.ANY)
    dma = pltpu.SemaphoreType.DMA
    q_slices, convolved = pl.pallas_call(
        kernel,
        out_shape=[jax.ShapeDtypeStruct((PIECE, slice_width), BF16)] * 2,
        in_specs=[hbm, hbm, hbm, hbm, hbm, vmem, hbm, hbm],
        out_specs=[anywhere, anywhere],
        scratch_shapes=[
            pltpu.VMEM((ROWS, width), BF16),
            pltpu.VMEM((ROWS, width), BF16),
            pltpu.VMEM((3, 3, width), F32),
            pltpu.VMEM((HALO, BLOCK, LANES), BF16),
            pltpu.VMEM(forward.shape, BF16),
            pltpu.VMEM(inverse.shape, BF16),
            pltpu.VMEM((2, 16, 512), BF16),
            pltpu.VMEM((2, 16, 512), BF16),
            pltpu.VMEM((2, 8, width), F32),
            pltpu.VMEM((PEERS, ROWS - HEAD, LANES), BF16),
            pltpu.VMEM((PEERS, HEAD, LANES), BF16),
            pltpu.VMEM((HALO_PIECES + PIECES, GROUPS, HEAD, LANES), BF16),
            pltpu.VMEM((16 + PIECE, slice_width), BF16),
            pltpu.VMEM((PIECE, slice_width), BF16),
            pltpu.VMEM((HALO + OWN, BLOCK, LANES), BF16),
            pltpu.VMEM((HALO + OWN, 2 * BLOCK, LANES), F32),
            pltpu.VMEM((HALO, 2 * BLOCK, LANES), F32),
            pltpu.VMEM((2, 2 * BLOCK, 2 * LANES), BF16),
            pltpu.VMEM((PIECES, PIECE, LANES), BF16),
            dma((6,)),
            dma((2,)),
            pltpu.SemaphoreType.REGULAR,
            dma((PEERS,)),
            dma((PEERS,)),
            dma((PEERS,)),
            dma((PIECES,)),
            dma((PIECES, GROUPS)),
            dma((PIECES,)),
            dma((PIECES,)),
            dma((PIECES,)),
            dma((GROUPS,)),
            dma((GROUPS,)),
            dma((2,)),
            dma((PIECES,)),
            dma((PIECES,)),
            dma((2,)),
        ],
        compiler_params=pltpu.CompilerParams(
            collective_id=0, has_side_effects=True, vmem_limit_bytes=VMEM_LIMIT
        ),
        cost_estimate=pl.CostEstimate(flops=9 * 10**9, bytes_accessed=16 * 2**20, transcendentals=0),
    )(
        queries,
        keys,
        values,
        short_filter,
        long_filter.reshape(HALO, BLOCK, slice_width),
        skip_gain,
        jnp.asarray(forward),
        jnp.asarray(inverse),
    )
    return (q_slices.astype(F32) * convolved.astype(F32)).astype(BF16)


def solution(mesh):
    return jax.shard_map(
        local,
        mesh=mesh,
        in_specs=(
            P(("stretch", "grp"), None),
            P(("stretch", "grp"), None),
            P(("stretch", "grp"), None),
            P(),
            P(None, "grp"),
            P("grp"),
        ),
        out_specs=P("stretch", "grp"),
        check_vma=False,
    )
```

time: 60 us -> 54.1 us (0.902)
  Pallas kernels: 57.1 us -> 50.8 us
    pallas_call x1, Pallas kernels: 57.1 us -> 50.8 us  [local(): pl.pallas_call(kernel, out_shape=[jax.ShapeDtypeStruct((PIECE, slice_widt...]
where the time goes in v2:
time: 54.1 us; the launch traced here: 53.6 us
  Pallas kernels  50.8 us (94%)
  other arithmetic  2.8 us (5%)
    pallas_call x1, Pallas kernels, local(): pl.pallas_call(kernel, out_shape=[jax.ShapeDtypeStruct((PIECE, slice_widt...  50.8 us
    convert_element_type x1, other arithmetic, local(): return (q_slices.astype(F32) * convolved.astype(F32)).astype(BF16)  2.8 us

profile of v2, /device:TPU:96, one launch (start us, length us, event | category | flops | bytes accessed | tf_op | source)
XLA Modules:
  0.0 53.6 jit_solution(10742061459726009133)
XLA Ops:
  0.0 50.8 %shard_map.82 = (bf16[1024,512]{1,0:T(8,128)(2,1)}, bf16[1024,512]{1,0:T(8,128)(2,1)}) custom-call(bf16[128,4096]{1,0:T(8,128)(2,1)} %queries.1, bf16[128,4096]{1,0:T(8,128)(2,1)} %keys.1, bf16[128,4096]{1,0:T(8,128)(2,1)} %values.1, f32[3,3,4096]{2,1,0:T(4,128)} %short_filter.1, bf16[6,512,512]{2,1,0:T(8,128)(2,1)} %bitcast.1, f32[512]{0:T(512)} %skip_gain.1, ...), custom_call_target="tpu_custom_call" | custom-call | flops 8999999488 | bytes 16777216 | tf_op jit(solution)/shard_map/pallas_call | solution.py:557
  50.8 2.8 %multiply_convert_fusion = bf16[1024,512]{1,0:T(8,128)(2,1)} fusion(bf16[1024,512]{1,0:T(8,128)(2,1)} %get-tuple-element.8, bf16[1024,512]{1,0:T(8,128)(2,1)} %get-tuple-element.7), kind=kLoop, calls=%fused_computation | loop fusion | flops 2097152 | bytes 3145728 | tf_op jit(solution)/shard_map/convert_element_type | solution.py:614

commit v3 on v2

--- a/solution.py
+++ b/solution.py
@@ -23,7 +23,8 @@
 AHEAD = 16
 PROMPT = 2
 BF16, F32 = jnp.bfloat16, jnp.float32
-Q_STEPS = (4, 6, 5, 7, 1, 3, 2)
+FAR = ((), (0, 2, 1, 3), (), (), (), (), (), ())
+NEAR = ((), (1, 3, 2), (), (), (), (), (), ())
 ORDER = (
     ("piece", 3),
     ("halo", 2),
@@ -64,6 +65,7 @@
     r_out,
     key_buf,
     value_buf,
+    query_buf,
     short_buf,
     filter_buf,
     forward,
@@ -74,8 +76,9 @@
     gated_buf,
     head_buf,
     heads,
-    q_raw,
     q_buf,
+    q_mid,
+    ones,
     signal,
     spectra,
     filter_spectra,
@@ -94,7 +97,8 @@
     halo_head_recv,
     q_send,
     q_recv,
-    q_edge_sem,
+    q_mid_send,
+    q_mid_recv,
     r_send,
     r_recv,
     own_sem,
@@ -102,16 +106,17 @@
     stretch, grp = lax.axis_index("stretch"), lax.axis_index("grp")
     plane, piece = lax.div(stretch, PIECES), lax.rem(stretch, PIECES)
     half, row = lax.div(grp, 4), lax.rem(grp, 4)
+    side, core = lax.div(piece, 2), lax.rem(piece, 2)
     has_before, has_after = plane > 0, plane < 3
     group_ends = grp == GROUPS - 1
     is_first = jnp.logical_and(stretch == 0, grp == 0)
     is_last = jnp.logical_and(stretch == 15, group_ends)
-    next_stretch = lax.rem(stretch + 1, 16)
 
     def peer(step, sign):
-        kp, ky, kx = lax.rem(step, 4), lax.rem(lax.div(step, 4), 4), lax.div(step, 16)
+        kp, ky, kx = lax.rem(step, 4), lax.div(step, 8), lax.rem(lax.div(step, 4), 2)
         p = lax.rem(piece + sign * kp + 4, 4)
-        y = lax.rem(row + sign * ky + 4, 4)
+        sender = core if sign > 0 else lax.rem(p, 2)
+        y = lax.rem(row + sign * ky * (1 - 2 * sender) + 4, 4)
         h = lax.rem(half + kx, 2)
         return p, h * 4 + y
 
@@ -129,8 +134,9 @@
         pltpu.make_async_copy(long_filter.at[:, :, own_lanes], filter_buf, load_sem.at[3]),
         pltpu.make_async_copy(forward_hbm, forward, load_sem.at[4]),
         pltpu.make_async_copy(inverse_hbm, inverse, load_sem.at[5]),
+        pltpu.make_async_copy(queries, query_buf, load_sem.at[6]),
     ]
-    for load in loads[:5]:
+    for load in loads[:3] + loads[6:] + loads[3:5]:
         load.start()
 
     barrier = pltpu.get_barrier_semaphore()
@@ -148,10 +154,6 @@
     def _():
         tell(stretch - PIECES, grp)
 
-    @pl.when(jnp.logical_and(has_before, piece == 0))
-    def _():
-        tell(stretch - 1, grp)
-
     @pl.when(jnp.logical_and(grp == 0, jnp.logical_not(is_first)))
     def _():
         tell(stretch - 1, GROUPS - 1)
@@ -162,9 +164,10 @@
 
     for load in loads[:3]:
         load.wait()
+    loads[6].wait()
     fold = 512
     row_at = lax.broadcasted_iota(jnp.int32, (16, fold), 0)
-    for n, buf in enumerate((key_buf, value_buf)):
+    for n, buf in enumerate((key_buf, value_buf, query_buf)):
         tail = buf[ROWS - 16 :, :].astype(F32)
         packed = jnp.zeros((16, fold), F32)
         for r in range(2):
@@ -217,7 +220,6 @@
         barrier,
         GROUPS - 1 + PIECES - 1
         + count(has_after)
-        + count(jnp.logical_and(has_after, piece == PIECES - 1))
         + count(jnp.logical_and(group_ends, jnp.logical_not(is_last))),
     )
     for s in pieces:
@@ -228,7 +230,7 @@
         edge_in,
         edge_sem.at[0],
         edge_sem.at[1],
-        device_id=(jnp.where(group_ends, next_stretch, stretch), jnp.where(group_ends, 0, grp + 1)),
+        device_id=(jnp.where(group_ends, lax.rem(stretch + 1, 16), stretch), jnp.where(group_ends, 0, grp + 1)),
         device_id_type=MESH,
     )
 
@@ -276,24 +278,6 @@
 
     lax.fori_loop(1, PEERS, send_rest, 0)
 
-    def q_copy(step):
-        other = lax.rem(half + step // 4, 2) * 4 + lax.rem(row + step % 4, 4)
-        return pltpu.make_async_remote_copy(
-            queries.at[:, aligned(other, 512)],
-            q_raw.at[pl.ds(pl.multiple_of(16 + grp * ROWS, 16), ROWS)],
-            q_send.at[step],
-            q_recv.at[step],
-            device_id=(stretch, other),
-            device_id_type=MESH,
-        )
-
-    own_q = pltpu.make_async_copy(
-        queries.at[:, aligned(grp, 512)],
-        q_raw.at[pl.ds(pl.multiple_of(16 + grp * ROWS, 16), ROWS)],
-        own_sem.at[0],
-    )
-    own_q.start()
-
     def transform(source, block, target, rows):
         pair = jnp.concatenate([source[block], source[block + 1]], axis=1)
         bins = jnp.dot(forward[rows, :], jnp.concatenate([pair, pair], axis=0), preferred_element_type=F32)
@@ -315,7 +299,7 @@
     def _():
         edge_copy.wait_recv()
 
-    for n in range(2):
+    for n in range(3):
         packed = edge_in[n].astype(F32)
         for r in range(2):
             for e in range(8):
@@ -330,6 +314,68 @@
     gate_first(0)
     own_head = pltpu.make_async_copy(head_buf.at[0], heads.at[HALO_PIECES + piece, grp], head_recv.at[piece])
     own_head.start()
+
+    def shorten_q(block, carry):
+        lanes = aligned(block, LANES)
+        now = query_buf[:, lanes].astype(F32)
+        q_buf[:, lanes] = shorten(now, edge[2, 0:1, lanes], edge[2, 1:2, lanes], 0, block).astype(BF16)
+        return carry
+
+    lax.fori_loop(0, PEERS, shorten_q, 0)
+    ones[...] = jnp.ones_like(ones)
+    q_rows = aligned(grp, ROWS)
+    side_lanes = aligned(side, 2 * LANES)
+    own_q = pltpu.make_async_copy(q_buf.at[:, aligned(grp, 512)], q_out.at[q_rows], own_sem.at[0])
+    ones_copy = pltpu.make_async_copy(
+        ones, q_out.at[aligned(1 - half, BLOCK), aligned(1 - side, 2 * LANES)], own_sem.at[2]
+    )
+
+    def q_near(step):
+        other = half * 4 + lax.rem(row + step, 4)
+        return pltpu.make_async_remote_copy(
+            q_buf.at[:, aligned(other, 512)],
+            q_out.at[q_rows],
+            q_send.at[step],
+            q_recv.at[step],
+            device_id=(stretch, other),
+            device_id_type=MESH,
+        )
+
+    def q_far(step):
+        other = (1 - half) * 4 + lax.rem(row + step, 4)
+        return pltpu.make_async_remote_copy(
+            q_buf.at[:, aligned(other * 2 + side, 2 * LANES)],
+            q_out.at[q_rows, side_lanes],
+            q_send.at[4 + step],
+            q_recv.at[4 + step],
+            device_id=(stretch, other),
+            device_id_type=MESH,
+        )
+
+    def q_aside(step):
+        k = step % 2
+        other, p = (1 - half) * 4 + lax.rem(row + step // 2, 4), 2 * (1 - side) + k
+        return pltpu.make_async_remote_copy(
+            q_buf.at[:, aligned(other * PIECES + p, LANES)],
+            q_mid.at[core, aligned(row, ROWS)],
+            q_mid_send.at[step],
+            q_mid_recv.at[core],
+            device_id=(plane * PIECES + p, other),
+            device_id_type=MESH,
+        )
+
+    for step in range(8):
+        q_aside(step).start()
+
+    def send_q(turn):
+        for step in FAR[turn]:
+            q_far(step).start()
+        for step in NEAR[turn]:
+            q_near(step).start()
+
+    own_q.start()
+    ones_copy.start()
+
     loads[5].start()
 
     def halo_copy(p, g):
@@ -389,15 +435,18 @@
                     for g in range(GROUPS):
                         halo_copy(p, g).start()
 
-    for step in Q_STEPS:
-        q_copy(step).start()
+    send_q(0)
     for p in (3, 2, 1, 0):
         settle(HALO_PIECES + p, HALO + 2 * p)
     transform_blocks(signal, spectra, HALO, PIECES)
 
     gain = skip_gain[own_lanes].reshape(1, LANES)
 
-    def convolve(p):
+    def wait_q_mid():
+        for c in range(2):
+            pltpu.make_async_copy(q_mid.at[c], q_mid.at[c], q_mid_recv.at[c]).wait()
+
+    def convolve(p, first):
         def bins(tile, carry):
             real, imag = aligned(tile, 16), pl.ds(pl.multiple_of(BLOCK + tile * 16, 16), 16)
             window = []
@@ -428,7 +477,19 @@
         back = jnp.dot(inverse[...], jnp.concatenate([high, low, high], axis=0), preferred_element_type=F32)
         for o in range(2):
             direct = gain * signal[HALO + 2 * p + o].astype(F32)
-            result[p, pl.ds(o * BLOCK, BLOCK)] = (back[:, o * LANES : (o + 1) * LANES] + direct).astype(BF16)
+            total = back[:, o * LANES : (o + 1) * LANES] + direct
+            here = jnp.logical_and(side != p // 2, half != o)
+
+            @pl.when(here)
+            def _():
+                if first:
+                    wait_q_mid()
+                result[p, pl.ds(o * BLOCK, BLOCK)] = (total * q_mid[p % 2].astype(F32)).astype(BF16)
+
+            @pl.when(jnp.logical_not(here))
+            def _():
+                result[p, pl.ds(o * BLOCK, BLOCK)] = total.astype(BF16)
+
 
     def r_copy(p):
         return pltpu.make_async_remote_copy(
@@ -462,52 +523,18 @@
         transform_blocks(signal, spectra, 2 * p, 1)
 
     loads[5].wait()
-    for what, p in ORDER:
+    sides = set()
+    for turn, (what, p) in enumerate(ORDER):
         if what == "halo":
             halo(p)
         else:
-            convolve(p)
+            convolve(p, p // 2 not in sides)
+            sides.add(p // 2)
             send_result(p)
+        send_q(1 + turn)
 
     own_q.wait()
-    for step in range(1, GROUPS):
-        q_copy(step).wait_recv()
-    q_edge = pltpu.make_async_remote_copy(
-        q_raw.at[pl.ds(PIECE, 16)],
-        q_raw.at[pl.ds(0, 16)],
-        q_edge_sem.at[0],
-        q_edge_sem.at[1],
-        device_id=(next_stretch, grp),
-        device_id_type=MESH,
-    )
-
-    @pl.when(stretch < 15)
-    def _():
-        q_edge.start()
-
-    @pl.when(stretch == 0)
-    def _():
-        q_raw[:16] = jnp.zeros((16, 512), BF16)
-
-    @pl.when(stretch > 0)
-    def _():
-        q_edge.wait_recv()
-
-    def shorten_q(unit, carry):
-        chunk, part = lax.div(unit, 4), lax.rem(unit, 4)
-        lanes = aligned(part, LANES)
-        now = q_raw[pl.ds(pl.multiple_of(16 + chunk * ROWS, 16), ROWS), lanes].astype(F32)
-        tail = q_raw[aligned(chunk, ROWS), lanes][:16].astype(F32)
-        q_buf[aligned(chunk, ROWS), lanes] = shorten(
-            now, tail[14:15], tail[15:16], 0, grp * 4 + part
-        ).astype(BF16)
-        return carry
-
-    lax.fori_loop(0, 32, shorten_q, 0)
-    q_copy_out = pltpu.make_async_copy(q_buf, q_out, own_sem.at[0])
-    q_copy_out.start()
-
-    q_copy_out.wait()
+    ones_copy.wait()
     own_r.wait()
     for p in range(PIECES):
 
@@ -517,12 +544,12 @@
             lanes = pl.ds(p * LANES, LANES)
             pltpu.make_async_copy(r_out.at[:, lanes], r_out.at[:, lanes], r_recv.at[p]).wait()
 
-    for step in range(1, GROUPS):
-        q_copy(step).wait_send()
-
-    @pl.when(stretch < 15)
-    def _():
-        q_edge.wait_send()
+    for step in range(1, 4):
+        q_near(step).wait()
+    for step in range(4):
+        q_far(step).wait()
+    for step in range(8):
+        q_aside(step).wait_send()
 
     @pl.when(jnp.logical_not(is_last))
     def _():
@@ -545,6 +572,10 @@
                 return carry
 
             lax.fori_loop(0, GROUPS, halo_sent, 0)
+
+
+def multiply(q_ref, r_ref, out_ref):
+    out_ref[...] = (q_ref[...].astype(F32) * r_ref[...].astype(F32)).astype(BF16)
 
 
 def local(queries, keys, values, short_filter, long_filter, skip_gain):
@@ -562,24 +593,26 @@
         scratch_shapes=[
             pltpu.VMEM((ROWS, width), BF16),
             pltpu.VMEM((ROWS, width), BF16),
+            pltpu.VMEM((ROWS, width), BF16),
             pltpu.VMEM((3, 3, width), F32),
             pltpu.VMEM((HALO, BLOCK, LANES), BF16),
             pltpu.VMEM(forward.shape, BF16),
             pltpu.VMEM(inverse.shape, BF16),
-            pltpu.VMEM((2, 16, 512), BF16),
-            pltpu.VMEM((2, 16, 512), BF16),
-            pltpu.VMEM((2, 8, width), F32),
+            pltpu.VMEM((3, 16, 512), BF16),
+            pltpu.VMEM((3, 16, 512), BF16),
+            pltpu.VMEM((3, 8, width), F32),
             pltpu.VMEM((PEERS, ROWS - HEAD, LANES), BF16),
             pltpu.VMEM((PEERS, HEAD, LANES), BF16),
             pltpu.VMEM((HALO_PIECES + PIECES, GROUPS, HEAD, LANES), BF16),
-            pltpu.VMEM((16 + PIECE, slice_width), BF16),
-            pltpu.VMEM((PIECE, slice_width), BF16),
+            pltpu.VMEM((ROWS, width), BF16),
+            pltpu.VMEM((2, BLOCK, LANES), BF16),
+            pltpu.VMEM((BLOCK, 2 * LANES), BF16),
             pltpu.VMEM((HALO + OWN, BLOCK, LANES), BF16),
             pltpu.VMEM((HALO + OWN, 2 * BLOCK, LANES), F32),
             pltpu.VMEM((HALO, 2 * BLOCK, LANES), F32),
             pltpu.VMEM((2, 2 * BLOCK, 2 * LANES), BF16),
             pltpu.VMEM((PIECES, PIECE, LANES), BF16),
-            dma((6,)),
+            dma((7,)),
             dma((2,)),
             pltpu.SemaphoreType.REGULAR,
             dma((PEERS,)),
@@ -592,10 +625,11 @@
             dma((PIECES,)),
             dma((GROUPS,)),
             dma((GROUPS,)),
+            dma((8,)),
             dma((2,)),
             dma((PIECES,)),
             dma((PIECES,)),
-            dma((2,)),
+            dma((3,)),
         ],
         compiler_params=pltpu.CompilerParams(
             collective_id=0, has_side_effects=True, vmem_limit_bytes=VMEM_LIMIT
@@ -611,7 +645,15 @@
         jnp.asarray(forward),
         jnp.asarray(inverse),
     )
-    return (q_slices.astype(F32) * convolved.astype(F32)).astype(BF16)
+    rows = PIECE // 2
+    part = pl.BlockSpec((rows, slice_width), lambda i: (i, 0))
+    return pl.pallas_call(
+        multiply,
+        out_shape=jax.ShapeDtypeStruct((PIECE, slice_width), BF16),
+        grid=(2,),
+        in_specs=[part, part],
+        out_specs=part,
+    )(q_slices, convolved)
 
 
 def solution(mesh):

time: 54.1 us -> 52 us (0.961)
  other arithmetic: 2.8 us -> 0 us
  Pallas kernels: 50.8 us -> 51.6 us
    convert_element_type x1 -> x0, other arithmetic: 2.8 us -> none  [local(): return (q_slices.astype(F32) * convolved.astype(F32)).astype(BF16)]
    pallas_call x0 -> x1, Pallas kernels: none -> 2.45 us  [local(): pl.pallas_call(multiply, out_shape=jax.ShapeDtypeStruct((PIECE, slice_wid...]
    pallas_call x1, Pallas kernels: 50.8 us -> 49.2 us  [local(): pl.pallas_call(kernel, out_shape=[jax.ShapeDtypeStruct((PIECE, slice_widt...]
where the time goes in v3:
time: 52 us; the launch traced here: 51.6 us
  Pallas kernels  51.6 us (99%)
    pallas_call x1, Pallas kernels, local(): pl.pallas_call(kernel, out_shape=[jax.ShapeDtypeStruct((PIECE, slice_widt...  49.2 us
    pallas_call x1, Pallas kernels, local(): pl.pallas_call(multiply, out_shape=jax.ShapeDtypeStruct((PIECE, slice_wid...  2.45 us

profile of v3, /device:TPU:96, one launch (start us, length us, event | category | flops | bytes accessed | tf_op | source)
XLA Modules:
  0.0 51.6 jit_solution(2758837829610852872)
XLA Ops:
  0.0 49.2 %shard_map.82 = (bf16[1024,512]{1,0:T(8,128)(2,1)}, bf16[1024,512]{1,0:T(8,128)(2,1)}) custom-call(bf16[128,4096]{1,0:T(8,128)(2,1)} %queries.1, bf16[128,4096]{1,0:T(8,128)(2,1)} %keys.1, bf16[128,4096]{1,0:T(8,128)(2,1)} %values.1, f32[3,3,4096]{2,1,0:T(4,128)} %short_filter.1, bf16[6,512,512]{2,1,0:T(8,128)(2,1)} %bitcast.1, f32[512]{0:T(512)} %skip_gain.1, ...), custom_call_target="tpu_custom_call" | custom-call | flops 8999999488 | bytes 16777216 | tf_op jit(solution)/shard_map/pallas_call | solution.py:588
  49.2 2.4 %shard_map.83 = bf16[1024,512]{1,0:T(8,128)(2,1)} custom-call(bf16[1024,512]{1,0:T(8,128)(2,1)} %get-tuple-element.7.q_ref, bf16[1024,512]{1,0:T(8,128)(2,1)} %get-tuple-element.8.r_ref), custom_call_target="tpu_custom_call" | custom-call | tf_op jit(solution)/shard_map/pallas_call | solution.py:650

commit v4 on v3

--- a/solution.py
+++ b/solution.py
@@ -20,11 +20,11 @@
 HALO = TAPS // BLOCK
 OWN = PIECES * PIECE // BLOCK
 HALO_PIECES = TAPS // PIECE
-AHEAD = 16
+AHEAD = 8
 PROMPT = 2
 BF16, F32 = jnp.bfloat16, jnp.float32
-FAR = ((), (0, 2, 1, 3), (), (), (), (), (), ())
-NEAR = ((), (1, 3, 2), (), (), (), (), (), ())
+FAR = ((0, 2), (1, 3), (), (), (), (), (), ())
+NEAR = ((1, 3, 2), (), (), (), (), (), (), ())
 ORDER = (
     ("piece", 3),
     ("halo", 2),
@@ -107,6 +107,7 @@
     plane, piece = lax.div(stretch, PIECES), lax.rem(stretch, PIECES)
     half, row = lax.div(grp, 4), lax.rem(grp, 4)
     side, core = lax.div(piece, 2), lax.rem(piece, 2)
+    around = 1 - 2 * core
     has_before, has_after = plane > 0, plane < 3
     group_ends = grp == GROUPS - 1
     is_first = jnp.logical_and(stretch == 0, grp == 0)
@@ -331,7 +332,7 @@
     )
 
     def q_near(step):
-        other = half * 4 + lax.rem(row + step, 4)
+        other = half * 4 + lax.rem(row + step * around + 4, 4)
         return pltpu.make_async_remote_copy(
             q_buf.at[:, aligned(other, 512)],
             q_out.at[q_rows],
@@ -342,7 +343,7 @@
         )
 
     def q_far(step):
-        other = (1 - half) * 4 + lax.rem(row + step, 4)
+        other = (1 - half) * 4 + lax.rem(row + step * around + 4, 4)
         return pltpu.make_async_remote_copy(
             q_buf.at[:, aligned(other * 2 + side, 2 * LANES)],
             q_out.at[q_rows, side_lanes],
@@ -354,7 +355,7 @@
 
     def q_aside(step):
         k = step % 2
-        other, p = (1 - half) * 4 + lax.rem(row + step // 2, 4), 2 * (1 - side) + k
+        other, p = (1 - half) * 4 + lax.rem(row + step // 2 * around + 4, 4), 2 * (1 - side) + k
         return pltpu.make_async_remote_copy(
             q_buf.at[:, aligned(other * PIECES + p, LANES)],
             q_mid.at[core, aligned(row, ROWS)],

time: 52 us -> 51.5 us (level)
    pallas_call x1, Pallas kernels: 49.2 us -> 48.6 us  [local(): pl.pallas_call(kernel, out_shape=[jax.ShapeDtypeStruct((PIECE, slice_widt...]
where the time goes in v4:
time: 51.5 us; the launch traced here: 51.1 us
  Pallas kernels  51.1 us (99%)
    pallas_call x1, Pallas kernels, local(): pl.pallas_call(kernel, out_shape=[jax.ShapeDtypeStruct((PIECE, slice_widt...  48.6 us
    pallas_call x1, Pallas kernels, local(): pl.pallas_call(multiply, out_shape=jax.ShapeDtypeStruct((PIECE, slice_wid...  2.45 us

profile of v4, /device:TPU:96, one launch (start us, length us, event | category | flops | bytes accessed | tf_op | source)
XLA Modules:
  0.0 51.1 jit_solution(7689051592843457790)
XLA Ops:
  0.0 48.6 %shard_map.82 = (bf16[1024,512]{1,0:T(8,128)(2,1)}, bf16[1024,512]{1,0:T(8,128)(2,1)}) custom-call(bf16[128,4096]{1,0:T(8,128)(2,1)} %queries.1, bf16[128,4096]{1,0:T(8,128)(2,1)} %keys.1, bf16[128,4096]{1,0:T(8,128)(2,1)} %values.1, f32[3,3,4096]{2,1,0:T(4,128)} %short_filter.1, bf16[6,512,512]{2,1,0:T(8,128)(2,1)} %bitcast.1, f32[512]{0:T(512)} %skip_gain.1, ...), custom_call_target="tpu_custom_call" | custom-call | flops 8999999488 | bytes 16777216 | tf_op jit(solution)/shard_map/pallas_call | solution.py:589
  48.6 2.4 %shard_map.83 = bf16[1024,512]{1,0:T(8,128)(2,1)} custom-call(bf16[1024,512]{1,0:T(8,128)(2,1)} %get-tuple-element.7.q_ref, bf16[1024,512]{1,0:T(8,128)(2,1)} %get-tuple-element.8.r_ref), custom_call_target="tpu_custom_call" | custom-call | tf_op jit(solution)/shard_map/pallas_call | solution.py:651

commit v5 on v4

--- a/solution.py
+++ b/solution.py
@@ -49,7 +49,7 @@
 
     high, low = parts(forward)
     back_high, back_low = parts(forward.T / BLOCK)
-    return np.concatenate([high, low], axis=1), np.concatenate([back_high, back_high, back_low], axis=1)
+    return np.concatenate([high, low], axis=1), np.concatenate([back_high, back_low], axis=1)
 
 
 def kernel(
@@ -467,15 +467,12 @@
                     re, im = fr * sr - fi * si, fr * si + fi * sr
                     sums[o] = (re, im) if sums[o] is None else (sums[o][0] + re, sums[o][1] + im)
             for n, at_rows in ((0, real), (1, imag)):
-                both = jnp.concatenate([sums[0][n], sums[1][n]], axis=1)
-                high = both.astype(BF16)
-                product[0, at_rows] = high
-                product[1, at_rows] = (both - high.astype(F32)).astype(BF16)
+                product[at_rows] = jnp.concatenate([sums[0][n], sums[1][n]], axis=1).astype(BF16)
             return carry
 
         lax.fori_loop(0, BLOCK // 16, bins, 0)
-        high, low = product[0], product[1]
-        back = jnp.dot(inverse[...], jnp.concatenate([high, low, high], axis=0), preferred_element_type=F32)
+        twice = jnp.concatenate([product[...], product[...]], axis=0)
+        back = jnp.dot(inverse[...], twice, preferred_element_type=F32)
         for o in range(2):
             direct = gain * signal[HALO + 2 * p + o].astype(F32)
             total = back[:, o * LANES : (o + 1) * LANES] + direct
@@ -611,7 +608,7 @@
             pltpu.VMEM((HALO + OWN, BLOCK, LANES), BF16),
             pltpu.VMEM((HALO + OWN, 2 * BLOCK, LANES), F32),
             pltpu.VMEM((HALO, 2 * BLOCK, LANES), F32),
-            pltpu.VMEM((2, 2 * BLOCK, 2 * LANES), BF16),
+            pltpu.VMEM((2 * BLOCK, 2 * LANES), BF16),
             pltpu.VMEM((PIECES, PIECE, LANES), BF16),
             dma((7,)),
             dma((2,)),

time: 51.5 us -> 50.5 us (0.981)
  the two profiles are of different devices: /device:TPU:96 before, /device:TPU:2 now
where the time goes in v5:
time: 50.5 us; the launch traced here: 50.3 us
  Pallas kernels  50.3 us (100%)
    pallas_call x1, Pallas kernels, local(): pl.pallas_call(kernel, out_shape=[jax.ShapeDtypeStruct((PIECE, slice_widt...  47.9 us
    pallas_call x1, Pallas kernels, local(): pl.pallas_call(multiply, out_shape=jax.ShapeDtypeStruct((PIECE, slice_wid...  2.45 us

profile of v5, /device:TPU:2, one launch (start us, length us, event | category | flops | bytes accessed | tf_op | source)
XLA Modules:
  0.0 50.3 jit_solution(8632229285001699529)
XLA Ops:
  0.0 47.9 %shard_map.82 = (bf16[1024,512]{1,0:T(8,128)(2,1)}, bf16[1024,512]{1,0:T(8,128)(2,1)}) custom-call(bf16[128,4096]{1,0:T(8,128)(2,1)} %queries.1, bf16[128,4096]{1,0:T(8,128)(2,1)} %keys.1, bf16[128,4096]{1,0:T(8,128)(2,1)} %values.1, f32[3,3,4096]{2,1,0:T(4,128)} %short_filter.1, bf16[6,512,512]{2,1,0:T(8,128)(2,1)} %bitcast.1, f32[512]{0:T(512)} %skip_gain.1, ...), custom_call_target="tpu_custom_call" | custom-call | flops 8999999488 | bytes 16777216 | tf_op jit(solution)/shard_map/pallas_call | solution.py:586
  47.9 2.4 %shard_map.83 = bf16[1024,512]{1,0:T(8,128)(2,1)} custom-call(bf16[1024,512]{1,0:T(8,128)(2,1)} %get-tuple-element.7.q_ref, bf16[1024,512]{1,0:T(8,128)(2,1)} %get-tuple-element.8.r_ref), custom_call_target="tpu_custom_call" | custom-call | tf_op jit(solution)/shard_map/pallas_call | solution.py:648

commit v6 on v5

--- a/solution.py
+++ b/solution.py
@@ -470,7 +470,7 @@
                 product[at_rows] = jnp.concatenate([sums[0][n], sums[1][n]], axis=1).astype(BF16)
             return carry
 
-        lax.fori_loop(0, BLOCK // 16, bins, 0)
+        lax.fori_loop(0, BLOCK // 16, bins, 0, unroll=2)
         twice = jnp.concatenate([product[...], product[...]], axis=0)
         back = jnp.dot(inverse[...], twice, preferred_element_type=F32)
         for o in range(2):

time: 50.5 us -> 50.5 us (level)
  no operation moved by 1% of the time
where the time goes in v6:
time: 50.5 us; the launch traced here: 50.3 us
  Pallas kernels  50.3 us (100%)
    pallas_call x1, Pallas kernels, local(): pl.pallas_call(kernel, out_shape=[jax.ShapeDtypeStruct((PIECE, slice_widt...  47.9 us
    pallas_call x1, Pallas kernels, local(): pl.pallas_call(multiply, out_shape=jax.ShapeDtypeStruct((PIECE, slice_wid...  2.45 us

profile of v6, /device:TPU:2, one launch (start us, length us, event | category | flops | bytes accessed | tf_op | source)
XLA Modules:
  0.0 50.3 jit_solution(16502075728269789463)
XLA Ops:
  0.0 47.9 %shard_map.82 = (bf16[1024,512]{1,0:T(8,128)(2,1)}, bf16[1024,512]{1,0:T(8,128)(2,1)}) custom-call(bf16[128,4096]{1,0:T(8,128)(2,1)} %queries.1, bf16[128,4096]{1,0:T(8,128)(2,1)} %keys.1, bf16[128,4096]{1,0:T(8,128)(2,1)} %values.1, f32[3,3,4096]{2,1,0:T(4,128)} %short_filter.1, bf16[6,512,512]{2,1,0:T(8,128)(2,1)} %bitcast.1, f32[512]{0:T(512)} %skip_gain.1, ...), custom_call_target="tpu_custom_call" | custom-call | flops 8999999488 | bytes 16777216 | tf_op jit(solution)/shard_map/pallas_call | solution.py:586
  47.9 2.4 %shard_map.83 = bf16[1024,512]{1,0:T(8,128)(2,1)} custom-call(bf16[1024,512]{1,0:T(8,128)(2,1)} %get-tuple-element.7.q_ref, bf16[1024,512]{1,0:T(8,128)(2,1)} %get-tuple-element.8.r_ref), custom_call_target="tpu_custom_call" | custom-call | tf_op jit(solution)/shard_map/pallas_call | solution.py:648
